TPU v7x, 256 devices: a whole 4x4x8 slice. The times are simulated.
256 devices in a mesh: grid: 32 (over y_lo, z, core), orb: 4 (over x), tau: 2 (over y_hi).
Axes of the slice: x: 4, y: 4 (y_hi: 2, y_lo: 2; y = y_hi * 2 + y_lo), z: 8, core: 2. Of those that a mesh axis runs over, the one named last changes fastest.
Arguments:
- green: bfloat16 [2, 6016, 6016], P('tau', 'grid', 'orb'), may hold values from -0.0009765625 to 0.0009765625
- colloc: bfloat16 [6016, 2048], P('grid', 'orb'), may hold values from -6 to 6
- core: bfloat16 [2048, 2048], P('grid', 'orb'), may hold values from -0.125 to 0.125
Outputs:
- sigma: bfloat16 [2, 6016, 6016], P('tau', 'grid', 'orb')
All inputs are finite; a program needn't handle non-finite values.
Results may differ from a plain program's by a relative error of at most 0.025.
Values may be sent and summed in bfloat16 or wider, within the bound.
No kernel may reach another device: no remote copies, remote signals or barrier semaphores. Data moves between devices by JAX's collectives and lax.ppermute only.
A program may use at most 64 MiB of HBM per device.

v0:
```python
import jax
import jax.numpy as jnp
from jax import lax
from jax.sharding import PartitionSpec as P


def partner(value, axis, distance):
    mask = 2**distance
    pairs = [(source, source ^ mask) for source in range(lax.axis_size(axis))]
    return lax.ppermute(value, axis, pairs)


def local(green, colloc, core):
    tile = green[0]
    row_panel, green_rows, core_rows = (
        lax.all_gather(colloc, "orb", axis=1, tiled=True),
        lax.all_gather(tile, "orb", axis=1, tiled=True),
        lax.all_gather(core, "orb", axis=1, tiled=True),
    )
    panel = lax.all_gather(colloc, "grid", axis=0, tiled=True)
    inner = jnp.dot(green_rows, panel, preferred_element_type=jnp.float32).astype(jnp.bfloat16)
    block = row_panel
    grid_tile = lax.psum_scatter(
        lax.dot_general(block, inner, (((0,), (0,)), ((), ())), preferred_element_type=jnp.float32),
        "grid",
        scatter_dimension=0,
        tiled=True,
    ).astype(jnp.bfloat16)
    other_time = partner(grid_tile, "tau", 0)
    pair = (grid_tile.astype(jnp.float32) * other_time.astype(jnp.float32)).astype(jnp.bfloat16)
    pair_rows = lax.all_gather(pair, "orb", axis=1, tiled=True)
    block = pair_rows
    left = jnp.dot(
        block, lax.all_gather(core, "grid", axis=0, tiled=True), preferred_element_type=jnp.float32
    ).astype(jnp.bfloat16)
    block = core_rows
    screened = jnp.dot(
        block, lax.all_gather(left, "grid", axis=0, tiled=True), preferred_element_type=jnp.float32
    )
    kernel = (grid_tile.astype(jnp.float32) * screened).astype(jnp.bfloat16)
    block = row_panel
    half = jnp.dot(
        block,
        lax.all_gather(kernel, "grid", axis=0, tiled=True),
        preferred_element_type=jnp.float32,
    ).astype(jnp.bfloat16)
    scale = -1.0 / row_panel.shape[1]
    partial_sigma = lax.dot_general(
        half, panel, (((1,), (1,)), ((), ())), preferred_element_type=jnp.float32
    )
    summed = lax.psum_scatter(
        partial_sigma.astype(jnp.bfloat16), "orb", scatter_dimension=1, tiled=True
    ).astype(jnp.float32)
    return (summed * scale).astype(jnp.bfloat16)[None]


def solution(mesh):
    placed = (P("tau", "grid", "orb"), P("grid", "orb"), P("grid", "orb"))
    return jax.shard_map(
        local, mesh=mesh, in_specs=placed, out_specs=P("tau", "grid", "orb"), check_vma=False
    )
```

profile of v0, /device:TPU:1, one launch (start us, length us, event | category | flops | bytes accessed | tf_op | source)
XLA Modules:
  0.0 552.8 jit_solution(4077504752122716853)
XLA Ops:
  6.5 4.7 copy.6
  12.1 12.9 %all_gather.26 = bf16[188,2048]{1,0:T(8,128)(2,1)S(1)} all-gather(bf16[188,512]{1,0:T(8,128)(2,1)S(1)} %copy-done), channel_id=1, replica_groups=mesh['grid'=32,'orb'=4,'tau'=2] {'orb'}, dimensions={1}, use_global_device_ids=true | all-gather | bytes 962560 | tf_op jit(solution)/shard_map/all_gather | solution.py:16
  25.1 57.3 %all-gather.14.cloned.1.call-done = bf16[1,188,6016]{1,0,2:T(2,128)(2,1)} async-done(((bf16[1,188,1504]{1,0,2:T(2,128)(2,1)}), bf16[1,188,6016]{1,0,2:T(2,128)(2,1)}) %all-gather.14.cloned.1.call-update) | async-done | bytes 2262032 | tf_op jit(solution)/shard_map/all_gather | solution.py:17
  82.4 13.9 %copy.7 = bf16[1,188,6016]{2,1,0:T(8,128)(2,1)S(1)} copy(bf16[1,188,6016]{1,0,2:T(2,128)(2,1)} %all-gather.14.cloned.1.call-done) | data formatting | bytes 4524032 | tf_op jit(solution)/shard_map/all_gather | solution.py:17
  96.3 59.3 %all-gather.16.cloned.1.call-done = bf16[32,188,512]{2,1,0:T(8,128)(2,1)} async-done(((bf16[1,188,512]{2,1,0:T(8,128)(2,1)}), bf16[32,188,512]{2,1,0:T(8,128)(2,1)}) %all-gather.16.cloned.1.call-update) | async-done | bytes 6160400 | tf_op jit(solution)/shard_map/all_gather | solution.py:20
  155.6 8.1 %reshape.2 = bf16[6016,512]{1,0:T(8,128)(2,1)} reshape(bf16[32,188,512]{2,1,0:T(8,128)(2,1)} %all-gather.16.cloned.1.call-done) | data formatting | bytes 12320768
  163.7 6.9 %convolution_bitcast_fusion = f32[2048,512]{0,1:T(8,128)} fusion(bf16[188,2048]{1,0:T(8,128)(2,1)S(1)} %all_gather.26, bf16[6016,512]{1,0:T(8,128)(2,1)} %reshape.2, bf16[1,188,6016]{2,1,0:T(8,128)(2,1)S(1)} %copy.7), kind=kOutput, calls=%fused_computation.1 | convolution fusion | flops 1552513024 | bytes 13386752 | tf_op jit(solution)/shard_map/dot_general | solution.py:24
  170.6 5.3 copy.9
  176.6 117.3 %reduce-scatter.7.cloned.1.call-done = f32[64,512]{1,0:T(8,128)} async-done(((f32[2048,512]{1,0:T(8,128)}), f32[64,512]{1,0:T(8,128)}) %reduce-scatter.7.cloned.1.call-update) | async-done | bytes 131088 | tf_op jit(solution)/shard_map/reduce_scatter | solution.py:23
  293.9 0.9 convert_element_type.36
  294.9 2.5 collective-permute-start
  297.4 2.2 collective-permute-done
  299.6 0.9 fusion.10
  300.5 9.7 %all_gather.27 = bf16[64,2048]{1,0:T(8,128)(2,1)S(1)} all-gather(bf16[64,512]{1,0:T(8,128)(2,1)S(1)} %fusion.10), channel_id=1, replica_groups=mesh['grid'=32,'orb'=4,'tau'=2] {'orb'}, dimensions={1}, use_global_device_ids=true | all-gather | bytes 327680 | tf_op jit(solution)/shard_map/all_gather | solution.py:31
  310.2 50.3 %all-gather.8.cloned.1.call-done = bf16[2048,512]{1,0:T(8,128)(2,1)} async-done(((bf16[64,512]{1,0:T(8,128)(2,1)}), bf16[2048,512]{1,0:T(8,128)(2,1)}) %all-gather.8.cloned.1.call-update) | async-done | bytes 2097168 | tf_op jit(solution)/shard_map/all_gather | solution.py:34
  360.4 2.7 convolution_convert_fusion.2
  363.2 10.3 %all_gather.30 = bf16[64,2048]{1,0:T(8,128)(2,1)S(1)} all-gather(bf16[64,512]{1,0:T(8,128)(2,1)S(1)} %copy-done.1), channel_id=1, replica_groups=mesh['grid'=32,'orb'=4,'tau'=2] {'orb'}, dimensions={1}, use_global_device_ids=true | all-gather | bytes 327680 | tf_op jit(solution)/shard_map/all_gather | solution.py:18
  373.5 54.2 %all-gather.10.cloned.1.call-done = bf16[2048,512]{1,0:T(8,128)(2,1)} async-done(((bf16[64,512]{1,0:T(8,128)(2,1)}), bf16[2048,512]{1,0:T(8,128)(2,1)}) %all-gather.10.cloned.1.call-update) | async-done | bytes 2097168 | tf_op jit(solution)/shard_map/all_gather | solution.py:38
  427.7 2.7 fusion.8
  430.5 64.5 %all-gather.12.cloned.1.call-done = bf16[2048,512]{1,0:T(8,128)(2,1)} async-done(((bf16[64,512]{1,0:T(8,128)(2,1)}), bf16[2048,512]{1,0:T(8,128)(2,1)}) %all-gather.12.cloned.1.call-update) | async-done | bytes 2097168 | tf_op jit(solution)/shard_map/all_gather | solution.py:44
  495.0 6.0 %convolution_convert_fusion = bf16[188,6016]{1,0:T(8,128)(2,1)S(1)} fusion(bf16[6016,512]{1,0:T(8,128)(2,1)} %reshape.2, bf16[2048,512]{1,0:T(8,128)(2,1)} %all-gather.12.cloned.1.call-done, bf16[188,2048]{1,0:T(8,128)(2,1)S(1)} %all_gather.26), kind=kOutput, calls=%fused_computation | convolution fusion | flops 1553644032 | bytes 11289600 | tf_op jit(solution)/shard_map/dot_general | solution.py:48
  501.0 2.9 copy.11
  503.9 39.8 %reduce-scatter.9.cloned.1.call-done = bf16[1504,188]{1,0:T(8,128)(2,1)} async-done(((bf16[6016,188]{1,0:T(8,128)(2,1)}), bf16[1504,188]{1,0:T(8,128)(2,1)}) %reduce-scatter.9.cloned.1.call-update) | async-done | bytes 565520
  543.7 1.4 copy.12
  (19 shorter events, 2.5 us)
Async XLA Ops:
  6.5 5.6 %copy-start = (bf16[188,512]{1,0:T(8,128)(2,1)S(1)}, bf16[188,512]{1,0:T(8,128)(2,1)}, u32[]{:S(2)}) copy-start(bf16[188,512]{1,0:T(8,128)(2,1)} %param.4) | copy-start | bytes 577540
  6.5 75.8 %all-gather.14.cloned.1.call-start = ((), (), s32[]{:S(2)}) async-start(), calls=%async_computation.5 | async-start | bytes 7700480 | tf_op jit(solution)/shard_map/all_gather | solution.py:17
  11.3 144.3 %all-gather.16.cloned.1.call-start = ((), (), s32[]{:S(2)}) async-start(), calls=%async_computation.6 | async-start | bytes 6488064 | tf_op jit(solution)/shard_map/all_gather | solution.py:20
  12.1 281.9 %reduce-scatter.7.cloned.1.call-start = ((), (), s32[]{:S(2)}) async-start(), calls=%async_computation.7 | async-start | bytes 4325376 | tf_op jit(solution)/shard_map/reduce_scatter | solution.py:23
  176.0 187.2 %copy-start.1 = (bf16[64,512]{1,0:T(8,128)(2,1)S(1)}, bf16[64,512]{1,0:T(8,128)(2,1)}, u32[]{:S(2)}) copy-start(bf16[64,512]{1,0:T(8,128)(2,1)} %param.5) | copy-start | bytes 196612
  176.0 184.4 %all-gather.8.cloned.1.call-start = ((), (), s32[]{:S(2)}) async-start(), calls=%async_computation.2 | async-start | bytes 2162688 | tf_op jit(solution)/shard_map/all_gather | solution.py:34
  176.6 251.1 %all-gather.10.cloned.1.call-start = ((), (), s32[]{:S(2)}) async-start(), calls=%async_computation.3 | async-start | bytes 2162688 | tf_op jit(solution)/shard_map/all_gather | solution.py:38
  294.9 4.7 collective-permute-start
  363.2 131.8 %all-gather.12.cloned.1.call-start = ((), (), s32[]{:S(2)}) async-start(), calls=%async_computation.4 | async-start | bytes 2162688 | tf_op jit(solution)/shard_map/all_gather | solution.py:44
  430.4 113.2 %reduce-scatter.9.cloned.1.call-start = ((), (), s32[]{:S(2)}) async-start(), calls=%async_computation.8 | async-start | bytes 3850240
Sparse Core Ops, SparseCore 0:
  11.4 70.8 all-gather.13
  84.2 71.3 all-gather.15
  176.1 117.7 reduce-scatter.6
  295.6 64.7 all-gather.7
  363.3 64.3 all-gather.9
  430.6 64.3 all-gather.11
  504.0 39.5 reduce-scatter.8
where the time goes:
time: 554 us; the launch traced here: 553 us
  waiting for transfers between devices  446 us (81%)
  local copies, waits for them, and re-layouts  36.4 us (7%)
  blocking collectives  32.9 us (6%)
  matrix products  18.4 us (3%)
  between operations  13.5 us (2%)
    reduce_scatter x1, waiting for transfers between devices, local(): lax.psum_scatter(lax.dot_general(block, inner, (((0,), (0,)), ((), ())),...  117 us
    all_gather x1, waiting for transfers between devices, local(): lax.all_gather(kernel, 'grid', axis=0, tiled=True)  64.5 us
    all_gather x1, waiting for transfers between devices, local(): panel = lax.all_gather(colloc, 'grid', axis=0, tiled=True)  59.3 us
    all_gather x1, waiting for transfers between devices, local(): lax.all_gather(tile, 'orb', axis=1, tiled=True)  57.3 us
    all_gather x1, waiting for transfers between devices, local(): lax.all_gather(left, 'grid', axis=0, tiled=True)  54.2 us
    all_gather x1, waiting for transfers between devices, local(): lax.all_gather(core, 'grid', axis=0, tiled=True)  50.3 us
    unnamed x8, waiting for transfers between devices  41.1 us
    unnamed x9, local copies, waits for them, and re-layouts  22.4 us
  transfers between devices with their start and end apart: 8, of which 8 were waited for; matrix products, arithmetic and copies ran while one was open for 3% of the time, Pallas kernels for 0%

commit v1 on v0

v1 whole, which is shorter than its diff:
```python
import jax
import jax.numpy as jnp
from jax import lax
from jax.sharding import Mesh
from jax.sharding import PartitionSpec as P

GRID = ("yl", "z", "c")
BF = jnp.bfloat16
F32 = jnp.float32


def swap(value, axes):
    return lax.all_to_all(value, axes, 0, 0, tiled=True)


def spread(value, axes):
    n = lax.axis_size(axes)
    return swap(jnp.broadcast_to(value[None], (n,) + value.shape), axes)


def shift(value, axis, by):
    n = lax.axis_size(axis)
    return lax.ppermute(value, axis, [(i, (i + by) % n) for i in range(n)])


def dot(a, b, ca, cb):
    return lax.dot_general(a, b, (((ca,), (cb,)), ((), ())), preferred_element_type=F32)


def local(green, colloc, core):
    nc, nx = lax.axis_size("c"), lax.axis_size("orb")
    c, x, tau = lax.axis_index("c"), lax.axis_index("orb"), lax.axis_index("tau")
    rows, cols = colloc.shape
    pad = 192
    half_cols = cols // 2
    quarter = cols // 4

    tile = green[0]
    chips = tile.shape[1] // (2 * rows)
    g0 = jnp.pad(tile.reshape(rows, chips, 2 * rows), ((0, 0), (0, 0), (0, 2 * pad - 2 * rows)))
    g0 = g0.reshape(rows, chips * 2 * pad)
    gs = [g0] + [shift(g0, "orb", d) for d in range(1, nx)]

    xpad = jnp.pad(colloc, ((0, pad - rows), (0, 0)))
    xrows = lax.all_gather(xpad, ("orb", "yl", "c"), axis=0, tiled=False)
    xrows = xrows.reshape(nx, 4 * pad, cols)
    zcols = lax.all_gather(core, GRID, axis=0, tiled=True)
    ycore = lax.dynamic_slice_in_dim(zcols, (2 * lax.axis_index("c") + lax.axis_index("yl")) * quarter, quarter, 1)
    zrows = lax.all_gather(core, ("yl", "c"), axis=0, tiled=True)
    zr = lax.dynamic_slice_in_dim(zrows, tau * 2 * core.shape[0], 2 * core.shape[0], 0)
    zr = lax.all_gather(zr, "orb", axis=1, tiled=True)

    split = jnp.stack([colloc[:, :half_cols], colloc[:, half_cols:]])
    mine = swap(split, "c").reshape(2 * rows, half_cols)
    mine = jnp.pad(mine, ((0, 2 * pad - 2 * rows), (0, 0)))
    panel = spread(mine, ("yl", "z"))
    panel = panel.reshape(nx, chips * 2 * pad, half_cols)

    gt = [shift(g, "c", 1) for g in gs]
    def inner_of(blocks):
        acc = 0.0
        for d in range(nx):
            acc = acc + dot(blocks[d], lax.dynamic_index_in_dim(panel, (x - d) % nx, 0, keepdims=False), 1, 0)
        return jnp.pad(acc.astype(BF), ((0, pad - rows), (0, 0)))
    own, other = inner_of(gs), inner_of(gt)
    inner = jnp.stack([jnp.where(c == 0, own, other), jnp.where(c == 0, other, own)])
    inner = swap(jnp.stack([inner[:, :, :quarter], inner[:, :, quarter:]]), "yl")
    inner = inner.reshape(4 * pad, quarter)

    part = lax.dot_general(xrows, inner, (((1,), (0,)), ((), ())), preferred_element_type=F32).astype(BF)
    part = part.reshape(2, 8, quarter, quarter)
    got = swap(part.reshape(16, quarter, quarter), ("tau", "z"))
    g = jnp.sum(got.reshape(2, 8, quarter, quarter).astype(F32), axis=1).astype(BF)
    gf = g.astype(F32)
    pair = (gf[0] * gf[1]).astype(BF)
    prow = spread(pair, ("orb", "c", "yl"))
    prow = jnp.transpose(prow, (1, 0, 2)).reshape(quarter, 16 * quarter)
    left = dot(prow, ycore, 1, 0).astype(BF)
    left = spread(left, ("tau", "z")).reshape(16 * quarter, quarter)
    screened = dot(zr, left, 1, 0)
    kern = (gf * screened[None]).astype(BF)
    send = jnp.broadcast_to(kern[:, None], (2, 8, quarter, quarter)).reshape(16, quarter, quarter)
    kt = swap(send, ("tau", "z"))
    kt = kt.reshape(nx, cols, quarter)
    half = 0.0
    for o in range(nx):
        half = half + dot(xrows[o], kt[o], 1, 0)
    half = half.astype(BF)
    send = jnp.broadcast_to(half.reshape(1, 2, 2, pad, quarter), (nx, 2, 2, pad, quarter))
    send = jnp.transpose(send, (0, 2, 1, 3, 4)).reshape(16, pad, quarter)
    hrow = swap(send, ("orb", "c", "yl"))
    hrow = jnp.transpose(hrow, (1, 0, 2)).reshape(pad, 16 * quarter)

    xj = swap(panel, "orb")
    xo = shift(xj, "c", 1)
    lo, hi = jnp.where(c == 0, xj, xo), jnp.where(c == 0, xo, xj)
    sig = 0.0
    h4 = hrow.reshape(pad, nx, 2, half_cols)
    for o in range(nx):
        sig = sig + dot(h4[:, o, 0], lo[o], 1, 1) + dot(h4[:, o, 1], hi[o], 1, 1)
    scale = -1.0 / (nx * cols)
    sig = (sig * scale).astype(BF)[:rows].reshape(rows, chips, 2 * pad)[:, :, : 2 * rows]
    return sig.reshape(1, rows, chips * 2 * rows)


def solution(mesh):
    fine = Mesh(mesh.devices.reshape(2, 8, 2, 4, 2), GRID + ("orb", "tau"))
    placed = (P("tau", GRID, "orb"), P(GRID, "orb"), P(GRID, "orb"))
    return jax.shard_map(
        local, mesh=fine, in_specs=placed, out_specs=P("tau", GRID, "orb"), check_vma=False
    )
```

time: 554 us -> 307 us (0.55)
  waiting for transfers between devices: 446 us -> 81.6 us
  blocking collectives: 32.9 us -> 118 us
  starting transfers between devices: 2.75 us -> 45.2 us
  local copies, waits for them, and re-layouts: 36.4 us -> 17.9 us
  matrix products: 18.4 us -> 24.8 us
    all_gather x5 -> x2, waiting for transfers between devices: 286 us -> 0.03 us  [the longest x1 0.02 us: local(): xrows = lax.all_gather(xpad, ('orb', 'yl', 'c'), axis=0, tiled=False)]
    reduce_scatter x1 -> x0, waiting for transfers between devices: 117 us -> none  [local(): lax.psum_scatter(lax.dot_general(block, inner, (((0,), (0,)), ((), ())),...]
    all_to_all x0 -> x4, blocking collectives: none -> 77.7 us  [swap(): return lax.all_to_all(value, axes, 0, 0, tiled=True)]
    all_to_all x0 -> x5, waiting for transfers between devices: none -> 48.9 us  [swap(): return lax.all_to_all(value, axes, 0, 0, tiled=True)]
    unnamed x8 -> x2, waiting for transfers between devices: 41.1 us -> 0.03 us
    all_to_all x0 -> x5, starting transfers between devices: none -> 30.9 us  [swap(): return lax.all_to_all(value, axes, 0, 0, tiled=True)]
    ppermute x1 -> x8, waiting for transfers between devices: 2.2 us -> 32.7 us  [shift(): return lax.ppermute(value, axis, [(i, (i + by) % n) for i in range(n)])]
    unnamed x9 -> x8, local copies, waits for them, and re-layouts: 22.4 us -> 0.32 us
  transfers between devices with their start and end apart: 8 -> 15, of which waited for: 8 -> 7; matrix products, arithmetic and copies ran while one was open for 3% -> 11% of each run, Pallas kernels for 0% -> 0%
where the time goes in v1:
time: 307 us; the launch traced here: 306 us
  blocking collectives  118 us (38%)
  waiting for transfers between devices  81.6 us (27%)
  starting transfers between devices  45.2 us (15%)
  matrix products  24.8 us (8%)
  local copies, waits for them, and re-layouts  17.9 us (6%)
  between operations  13.9 us (5%)
  other arithmetic  3.82 us (1%)
    all_to_all x4, blocking collectives, swap(): return lax.all_to_all(value, axes, 0, 0, tiled=True)  77.7 us
    all_to_all x5, waiting for transfers between devices, swap(): return lax.all_to_all(value, axes, 0, 0, tiled=True)  48.9 us
    ppermute x8, waiting for transfers between devices, shift(): return lax.ppermute(value, axis, [(i, (i + by) % n) for i in range(n)])  32.7 us
    all_gather x1, blocking collectives, local(): zr = lax.all_gather(zr, 'orb', axis=1, tiled=True)  32.4 us
    all_to_all x5, starting transfers between devices, swap(): return lax.all_to_all(value, axes, 0, 0, tiled=True)  30.9 us
    dot_general x22, matrix products, dot(): lax.dot_general(a, b, (((ca,), (cb,)), ((), ())), preferred_element_type=...  21.9 us
    ppermute x8, starting transfers between devices, shift(): return lax.ppermute(value, axis, [(i, (i + by) % n) for i in range(n)])  14.2 us
    all_gather x1, blocking collectives, local(): zrows = lax.all_gather(core, ('yl', 'c'), axis=0, tiled=True)  8.39 us
  transfers between devices with their start and end apart: 15, of which 7 were waited for; matrix products, arithmetic and copies ran while one was open for 11% of the time, Pallas kernels for 0%

profile of v1, /device:TPU:1, one launch (start us, length us, event | category | flops | bytes accessed | tf_op | source)
XLA Modules:
  0.0 305.7 jit_solution(9422497091914118904)
XLA Ops:
  9.2 6.8 %all_to_all.45 = bf16[2,188,256]{2,1,0:T(8,128)(2,1)S(1)} all-to-all(bf16[2,188,256]{2,1,0:T(8,128)(2,1)S(1)} %pad_maximum_fusion), channel_id=1, replica_groups=mesh['yl'=2,'z'=8,'c'=2,'orb'=4,'tau'=2] {'c'}, dimensions={0} | all-to-all | bytes 385024 | tf_op jit(solution)/shard_map/all_to_all | solution.py:13
  16.0 2.0 broadcast_in_dim.14
  18.0 7.7 %all-to-all-start.1 = ((bf16[16,384,256]{2,1,0:T(8,128)(2,1)}), bf16[16,384,256]{2,1,0:T(8,128)(2,1)}, u32[]{:S(2)}, u32[]{:S(2)}) async-start(bf16[16,384,256]{2,1,0:T(8,128)(2,1)} %broadcast_in_dim.14), calls=%async_computation.1 | async-start | bytes 6291456 | tf_op jit(solution)/shard_map/all_to_all | solution.py:13
  32.9 12.8 %collective-permute-done = bf16[188,1536]{1,0:T(8,128)(2,1)S(1)} collective-permute-done((bf16[188,1536]{1,0:T(8,128)(2,1)S(1)}, bf16[188,1536]{1,0:T(8,128)(2,1)S(1)}, u32[]{:S(2)}, u32[]{:S(2)}) %collective-permute-start) | collective-permute-done | bytes 577568 | tf_op jit(solution)/shard_map/ppermute | solution.py:23
  48.9 1.8 collective-permute-start.6
  50.7 18.2 %collective-permute-done.1 = bf16[188,1536]{1,0:T(8,128)(2,1)S(1)} collective-permute-done((bf16[188,1536]{1,0:T(8,128)(2,1)S(1)}, bf16[188,1536]{1,0:T(8,128)(2,1)S(1)}, u32[]{:S(2)}, u32[]{:S(2)}) %collective-permute-start.1) | collective-permute-done | bytes 577568 | tf_op jit(solution)/shard_map/ppermute | solution.py:23
  69.4 26.4 %all-to-all-done.1 = bf16[16,384,256]{2,1,0:T(8,128)(2,1)} async-done(((bf16[16,384,256]{2,1,0:T(8,128)(2,1)}), bf16[16,384,256]{2,1,0:T(8,128)(2,1)}, u32[]{:S(2)}, u32[]{:S(2)}) %all-to-all-start.1) | async-done | bytes 3145760 | tf_op jit(solution)/shard_map/all_to_all | solution.py:13
  108.7 3.4 %all-to-all-start.2 = ((bf16[2,2,192,128]{3,2,1,0:T(8,128)(2,1)}), bf16[2,2,192,128]{3,2,1,0:T(8,128)(2,1)S(1)}, u32[]{:S(2)}, u32[]{:S(2)}) async-start(bf16[2,2,192,128]{3,2,1,0:T(8,128)(2,1)} %pad_maximum_fusion.1), calls=%async_computation.2 | async-start | bytes 393216 | tf_op jit(solution)/shard_map/all_to_all | solution.py:13
  112.2 4.3 %all-to-all-done.2 = bf16[2,2,192,128]{3,2,1,0:T(8,128)(2,1)S(1)} async-done(((bf16[2,2,192,128]{3,2,1,0:T(8,128)(2,1)}), bf16[2,2,192,128]{3,2,1,0:T(8,128)(2,1)S(1)}, u32[]{:S(2)}, u32[]{:S(2)}) %all-to-all-start.2) | async-done | bytes 196640 | tf_op jit(solution)/shard_map/all_to_all | solution.py:13
  116.5 2.9 convolution_convert_fusion
  119.5 28.5 %all_to_all.46 = bf16[16,128,128]{2,1,0:T(8,128)(2,1)S(1)} all-to-all(bf16[16,128,128]{2,1,0:T(8,128)(2,1)S(1)} %bitcast.138), channel_id=1, replica_groups=mesh['yl'=2,'z'=8,'c'=2,'orb'=4,'tau'=2] {'tau','z'}, dimensions={0} | all-to-all | bytes 1048576 | tf_op jit(solution)/shard_map/all_to_all | solution.py:13
  149.0 7.5 %all-to-all-start.4 = ((bf16[16,128,128]{1,2,0:T(8,128)(2,1)}), bf16[16,128,128]{1,2,0:T(8,128)(2,1)S(1)}, u32[]{:S(2)}, u32[]{:S(2)}) async-start(bf16[16,128,128]{1,2,0:T(8,128)(2,1)} %broadcast_in_dim.16), calls=%async_computation.4 | async-start | bytes 1048576 | tf_op jit(solution)/shard_map/all_to_all | solution.py:13
  156.5 11.0 %all-to-all-done.4 = bf16[16,128,128]{1,2,0:T(8,128)(2,1)S(1)} async-done(((bf16[16,128,128]{1,2,0:T(8,128)(2,1)}), bf16[16,128,128]{1,2,0:T(8,128)(2,1)S(1)}, u32[]{:S(2)}, u32[]{:S(2)}) %all-to-all-start.4) | async-done | bytes 524320 | tf_op jit(solution)/shard_map/all_to_all | solution.py:13
  169.0 19.5 %all_to_all.47 = bf16[16,128,128]{2,1,0:T(8,128)(2,1)} all-to-all(bf16[16,128,128]{2,1,0:T(8,128)(2,1)S(1)} %broadcast_in_dim.17), channel_id=1, replica_groups=mesh['yl'=2,'z'=8,'c'=2,'orb'=4,'tau'=2] {'tau','z'}, dimensions={0} | all-to-all | bytes 1048576 | tf_op jit(solution)/shard_map/all_to_all | solution.py:13
  188.6 3.8 %all-to-all-start.8 = ((bf16[4,1536,256]{2,1,0:T(8,128)(2,1)}), bf16[4,1536,256]{2,1,0:T(8,128)(2,1)S(1)}, u32[]{:S(2)}, u32[]{:S(2)}) async-start(bf16[4,1536,256]{2,1,0:T(8,128)(2,1)} %bitcast.3), calls=%async_computation.8 | async-start | bytes 6291456 | tf_op jit(solution)/shard_map/all_to_all | solution.py:13
  192.4 8.4 %all_gather.17 = bf16[256,512]{1,0:T(8,128)(2,1)S(1)} all-gather(bf16[64,512]{1,0:T(8,128)(2,1)S(1)} %copy-done.2), channel_id=1, replica_groups=mesh['yl'=2,'z'=8,'c'=2,'orb'=4,'tau'=2] {'yl','c'}, dimensions={0}, use_global_device_ids=true | all-gather | bytes 327680 | tf_op jit(solution)/shard_map/all_gather | solution.py:49
  200.8 32.4 %all_gather.18 = bf16[128,2048]{1,0:T(8,128)(2,1)S(1)} all-gather(bf16[128,512]{1,0:T(8,128)(2,1)S(1)} %constant_dynamic-slice_fusion), channel_id=1, replica_groups=mesh['yl'=2,'z'=8,'c'=2,'orb'=4,'tau'=2] {'orb'}, dimensions={1}, use_global_device_ids=true | all-gather | bytes 655360 | tf_op jit(solution)/shard_map/all_gather | solution.py:51
  235.4 8.4 %all-to-all-start.6 = ((bf16[16,128,128]{2,1,0:T(8,128)(2,1)}), bf16[16,128,128]{2,1,0:T(8,128)(2,1)}, u32[]{:S(2)}, u32[]{:S(2)}) async-start(bf16[16,128,128]{2,1,0:T(8,128)(2,1)} %bitcast.137), calls=%async_computation.6 | async-start | bytes 1048576 | tf_op jit(solution)/shard_map/all_to_all | solution.py:13
  243.9 4.7 %collective-permute-start.7 = (bf16[4,1536,256]{2,1,0:T(8,128)(2,1)S(1)}, bf16[4,1536,256]{2,1,0:T(8,128)(2,1)}, u32[]{:S(2)}, u32[]{:S(2)}) collective-permute-start(bf16[4,1536,256]{2,1,0:T(8,128)(2,1)S(1)} %all-to-all-done.8), channel_id=1, source_target_pairs={{0,8},{8,0},{1,9},{9,1},{2,10},{10,2},{3,11},{11,3},{4,12},{12,4},... | collective-permute-start | bytes 9437192 | tf_op jit(solution)/shard_map/ppermute | solution.py:23
  248.6 7.2 %all-to-all-done.6 = bf16[16,128,128]{2,1,0:T(8,128)(2,1)} async-done(((bf16[16,128,128]{2,1,0:T(8,128)(2,1)}), bf16[16,128,128]{2,1,0:T(8,128)(2,1)}, u32[]{:S(2)}, u32[]{:S(2)}) %all-to-all-start.6) | async-done | bytes 524320 | tf_op jit(solution)/shard_map/all_to_all | solution.py:13
  261.0 22.9 %all_to_all.48 = bf16[16,192,128]{2,1,0:T(8,128)(2,1)S(1)} all-to-all(bf16[16,192,128]{2,1,0:T(8,128)(2,1)S(1)} %bitcast.127), channel_id=1, replica_groups=mesh['yl'=2,'z'=8,'c'=2,'orb'=4,'tau'=2] {'orb','c','yl'}, dimensions={0} | all-to-all | bytes 1572864 | tf_op jit(solution)/shard_map/all_to_all | solution.py:13
  285.3 2.9 reshape_reshape.7
  288.2 2.9 fusion.72
  291.1 2.3 broadcast_select_fusion.1
  (75 shorter events, 43.1 us)
Async XLA Ops:
  6.5 105.6 %all-gather.6.cloned.1.call-start = ((), (), s32[]{:S(2)}) async-start(), calls=%async_computation.10 | async-start | bytes 3342336 | tf_op jit(solution)/shard_map/all_gather | solution.py:45
  18.0 7.8 %copy-start.1 = (bf16[1,188,1504]{2,1,0:T(8,128)(2,1)S(1)}, bf16[1,188,1504]{2,1,0:T(8,128)(2,1)}, u32[]{:S(2)}) copy-start(bf16[1,188,1504]{2,1,0:T(8,128)(2,1)} %param.3) | copy-start | bytes 1696516
  18.0 77.7 %all-to-all-start.1 = ((bf16[16,384,256]{2,1,0:T(8,128)(2,1)}), bf16[16,384,256]{2,1,0:T(8,128)(2,1)}, u32[]{:S(2)}, u32[]{:S(2)}) async-start(bf16[16,384,256]{2,1,0:T(8,128)(2,1)} %broadcast_in_dim.14), calls=%async_computation.1 | async-start | bytes 6291456 | tf_op jit(solution)/shard_map/all_to_all | solution.py:13
  25.8 130.7 %all-gather.4.cloned.1.call-start = ((), (), s32[]{:S(2)}) async-start(), calls=%async_computation.9 | async-start | bytes 2162688 | tf_op jit(solution)/shard_map/all_gather | solution.py:47
  27.0 18.7 %collective-permute-start = (bf16[188,1536]{1,0:T(8,128)(2,1)S(1)}, bf16[188,1536]{1,0:T(8,128)(2,1)S(1)}, u32[]{:S(2)}, u32[]{:S(2)}) collective-permute-start(bf16[188,1536]{1,0:T(8,128)(2,1)S(1)} %bitcast.128), channel_id=1, source_target_pairs={{0,2},{2,4},{4,6},{6,0},{1,3},{3,5},{5,7},{7,1},{8,10},{10,12},{12... | collective-permute-start | bytes 1732616 | tf_op jit(solution)/shard_map/ppermute | solution.py:23
  28.3 20.6 %collective-permute-start.2 = (bf16[188,1536]{1,0:T(8,128)(2,1)S(1)}, bf16[188,1536]{1,0:T(8,128)(2,1)S(1)}, u32[]{:S(2)}, u32[]{:S(2)}) collective-permute-start(bf16[188,1536]{1,0:T(8,128)(2,1)S(1)} %bitcast.129), channel_id=1, source_target_pairs={{0,6},{2,0},{4,2},{6,4},{1,7},{3,1},{5,3},{7,5},{8,14},{10,8},{12,... | collective-permute-start | bytes 1732616 | tf_op jit(solution)/shard_map/ppermute | solution.py:23
  29.8 39.0 %collective-permute-start.1 = (bf16[188,1536]{1,0:T(8,128)(2,1)S(1)}, bf16[188,1536]{1,0:T(8,128)(2,1)S(1)}, u32[]{:S(2)}, u32[]{:S(2)}) collective-permute-start(bf16[188,1536]{1,0:T(8,128)(2,1)S(1)} %bitcast.130), channel_id=1, source_target_pairs={{0,4},{2,6},{4,0},{6,2},{1,5},{3,7},{5,1},{7,3},{8,12},{10,14},{12... | collective-permute-start | bytes 1732616 | tf_op jit(solution)/shard_map/ppermute | solution.py:23
  31.3 67.3 %collective-permute-start.3 = (bf16[188,1536]{1,0:T(8,128)(2,1)S(1)}, bf16[188,1536]{1,0:T(8,128)(2,1)S(1)}, u32[]{:S(2)}, u32[]{:S(2)}) collective-permute-start(bf16[188,1536]{1,0:T(8,128)(2,1)S(1)} %bitcast.131), channel_id=1, source_target_pairs={{0,8},{8,0},{1,9},{9,1},{2,10},{10,2},{3,11},{11,3},{4,12},{12,4},... | collective-permute-start | bytes 1732616 | tf_op jit(solution)/shard_map/ppermute | solution.py:23
  45.7 57.4 %collective-permute-start.4 = (bf16[188,1536]{1,0:T(8,128)(2,1)S(1)}, bf16[188,1536]{1,0:T(8,128)(2,1)}, u32[]{:S(2)}, u32[]{:S(2)}) collective-permute-start(bf16[188,1536]{1,0:T(8,128)(2,1)S(1)} %collective-permute-done), channel_id=1, source_target_pairs={{0,8},{8,0},{1,9},{9,1},{2,10},{10,2},{3,11},{11,3},{4,12},{12,4},... | collective-permute-start | bytes 1732616 | tf_op jit(solution)/shard_map/ppermute | solution.py:23
  48.9 52.7 %collective-permute-start.6 = (bf16[188,1536]{1,0:T(8,128)(2,1)S(1)}, bf16[188,1536]{1,0:T(8,128)(2,1)S(1)}, u32[]{:S(2)}, u32[]{:S(2)}) collective-permute-start(bf16[188,1536]{1,0:T(8,128)(2,1)S(1)} %collective-permute-done.2), channel_id=1, source_target_pairs={{0,8},{8,0},{1,9},{9,1},{2,10},{10,2},{3,11},{11,3},{4,12},{12,4},... | collective-permute-start | bytes 1732616 | tf_op jit(solution)/shard_map/ppermute | solution.py:23
  68.8 37.4 %collective-permute-start.5 = (bf16[188,1536]{1,0:T(8,128)(2,1)S(1)}, bf16[188,1536]{1,0:T(8,128)(2,1)}, u32[]{:S(2)}, u32[]{:S(2)}) collective-permute-start(bf16[188,1536]{1,0:T(8,128)(2,1)S(1)} %collective-permute-done.1), channel_id=1, source_target_pairs={{0,8},{8,0},{1,9},{9,1},{2,10},{10,2},{3,11},{11,3},{4,12},{12,4},... | collective-permute-start | bytes 1732616 | tf_op jit(solution)/shard_map/ppermute | solution.py:23
  108.7 7.8 %all-to-all-start.2 = ((bf16[2,2,192,128]{3,2,1,0:T(8,128)(2,1)}), bf16[2,2,192,128]{3,2,1,0:T(8,128)(2,1)S(1)}, u32[]{:S(2)}, u32[]{:S(2)}) async-start(bf16[2,2,192,128]{3,2,1,0:T(8,128)(2,1)} %pad_maximum_fusion.1), calls=%async_computation.2 | async-start | bytes 393216 | tf_op jit(solution)/shard_map/all_to_all | solution.py:13
  149.0 18.5 %all-to-all-start.4 = ((bf16[16,128,128]{1,2,0:T(8,128)(2,1)}), bf16[16,128,128]{1,2,0:T(8,128)(2,1)S(1)}, u32[]{:S(2)}, u32[]{:S(2)}) async-start(bf16[16,128,128]{1,2,0:T(8,128)(2,1)} %broadcast_in_dim.16), calls=%async_computation.4 | async-start | bytes 1048576 | tf_op jit(solution)/shard_map/all_to_all | solution.py:13
  188.6 3.8 %copy-start.2 = (bf16[64,512]{1,0:T(8,128)(2,1)S(1)}, bf16[64,512]{1,0:T(8,128)(2,1)}, u32[]{:S(2)}) copy-start(bf16[64,512]{1,0:T(8,128)(2,1)} %param.5) | copy-start | bytes 196612
  188.6 46.0 %all-to-all-start.8 = ((bf16[4,1536,256]{2,1,0:T(8,128)(2,1)}), bf16[4,1536,256]{2,1,0:T(8,128)(2,1)S(1)}, u32[]{:S(2)}, u32[]{:S(2)}) async-start(bf16[4,1536,256]{2,1,0:T(8,128)(2,1)} %bitcast.3), calls=%async_computation.8 | async-start | bytes 6291456 | tf_op jit(solution)/shard_map/all_to_all | solution.py:13
  235.4 20.3 %all-to-all-start.6 = ((bf16[16,128,128]{2,1,0:T(8,128)(2,1)}), bf16[16,128,128]{2,1,0:T(8,128)(2,1)}, u32[]{:S(2)}, u32[]{:S(2)}) async-start(bf16[16,128,128]{2,1,0:T(8,128)(2,1)} %bitcast.137), calls=%async_computation.6 | async-start | bytes 1048576 | tf_op jit(solution)/shard_map/all_to_all | solution.py:13
  243.9 47.2 %collective-permute-start.7 = (bf16[4,1536,256]{2,1,0:T(8,128)(2,1)S(1)}, bf16[4,1536,256]{2,1,0:T(8,128)(2,1)}, u32[]{:S(2)}, u32[]{:S(2)}) collective-permute-start(bf16[4,1536,256]{2,1,0:T(8,128)(2,1)S(1)} %all-to-all-done.8), channel_id=1, source_target_pairs={{0,8},{8,0},{1,9},{9,1},{2,10},{10,2},{3,11},{11,3},{4,12},{12,4},... | collective-permute-start | bytes 9437192 | tf_op jit(solution)/shard_map/ppermute | solution.py:23
  255.8 4.3 %copy-start = (bf16[3072,512]{1,0:T(8,128)(2,1)S(1)}, bf16[3072,512]{1,0:T(8,128)(2,1)}, u32[]{:S(2)}) copy-start(bf16[3072,512]{1,0:T(8,128)(2,1)} %all-gather.6.cloned.1.call-done) | copy-start | bytes 9437188
Sparse Core Ops, SparseCore 0:
  9.2 55.6 all-gather.5
  66.8 79.5 all-gather.3

commit v2 on v1

v2 whole, which is shorter than its diff:
```python
import functools

import jax
import jax.numpy as jnp
from jax import lax
from jax.experimental import pallas as pl
from jax.experimental.pallas import tpu as pltpu
from jax.sharding import Mesh
from jax.sharding import PartitionSpec as P

GRID = ("yl", "z", "c")
BF = jnp.bfloat16
F32 = jnp.float32
VMEM = 56 * 2**20


def swap(value, axes):
    return lax.all_to_all(value, axes, 0, 0, tiled=True)


def spread(value, axes):
    n = lax.axis_size(axes)
    return swap(jnp.broadcast_to(value[None], (n,) + value.shape), axes)


def shift(value, axis, by):
    n = lax.axis_size(axis)
    return lax.ppermute(value, axis, [(i, (i + by) % n) for i in range(n)])


def dot(a, b, ca, cb):
    return lax.dot_general(a, b, (((ca,), (cb,)), ((), ())), preferred_element_type=F32)


def fetch(pairs, sems):
    copies = [pltpu.make_async_copy(s, d, sems.at[i]) for i, (s, d) in enumerate(pairs)]
    for copy in copies:
        copy.start()
    return copies


def ring_places(z, n):
    return [z] + [lax.rem(z - d + n, n) for d in (1, 2, 3, 4)] + [lax.rem(z + d, n) for d in (1, 2, 3)]


def inner_kernel(second, place, own, other, *refs):
    ring, refs = refs[:8], refs[8:]
    if second:
        before, refs = refs[0], refs[1:]
    out, zc, rows_out, xbuf, xsem, osem = refs
    yl, z = place[1], place[3]
    copies = fetch([(r, xbuf.at[p]) for r, p in zip(ring, ring_places(z, 8))], xsem)
    if second:
        for k in range(2):
            out[2 * (1 - yl) + k] = before[k]
    for copy in copies:
        copy.wait()
    rows, width = own.shape[0], out.shape[4]
    store = pltpu.make_async_copy(xbuf.at[:, :, pl.ds(0, rows)], rows_out, osem)
    store.start()
    for k in range(2):
        panel = xbuf[4 * k : 4 * k + 4, :, :rows].reshape(own.shape[1], 2 * width)
        for side, block in enumerate((own, other)):
            term = dot(block[...], panel, 1, 0).astype(BF)
            for part in range(2):
                out[2 * yl + k if second else k, part, side] = term[:, part * width : (part + 1) * width]
    cols = pl.ds(pl.multiple_of(place[4] * width, width), width)
    zc[...] = xbuf[:, :, rows:, cols].reshape(zc.shape)
    store.wait()


def half_kernel(blocks, kt, out):
    pad = out.shape[1]
    for q in range(4):
        acc = None
        for o in range(kt.shape[0]):
            term = dot(blocks[o, q, :pad], kt[o], 1, 0)
            acc = term if acc is None else acc + term
        out[2 * (q % 2) + q // 2] = acc.astype(BF)


ANY = pl.BlockSpec(memory_space=pl.ANY)
SMEM = pl.BlockSpec(memory_space=pltpu.SMEM)
VM = pl.BlockSpec(memory_space=pltpu.VMEM)


def inner_call(place, own, other, ring, before=None):
    rows, k = own.shape
    deep, width = ring[0].shape[1:]
    second = before is not None
    count = 4 if second else 2
    return pl.pallas_call(
        functools.partial(inner_kernel, second),
        out_shape=(
            jax.ShapeDtypeStruct((count, 2, 2, rows, width // 2), BF),
            jax.ShapeDtypeStruct((16 * (deep - rows), width // 2), BF),
            jax.ShapeDtypeStruct((8, 2, rows, width), BF),
        ),
        in_specs=[SMEM, VM, VM] + [ANY] * 8 + [VM] * second,
        out_specs=(VM, VM, ANY),
        scratch_shapes=[
            pltpu.VMEM((8, 2, deep, width), BF),
            pltpu.SemaphoreType.DMA((8,)),
            pltpu.SemaphoreType.DMA,
        ],
        compiler_params=pltpu.CompilerParams(vmem_limit_bytes=VMEM),
        cost_estimate=pl.CostEstimate(flops=8 * rows * k * width, bytes_accessed=6 * 2**20, transcendentals=0),
        name="inner",
    )(place, own, other, *ring, *([before] if second else []))


def half_call(blocks, kt, pad):
    width = kt.shape[2]
    return pl.pallas_call(
        half_kernel,
        out_shape=jax.ShapeDtypeStruct((4, pad, width), BF),
        in_specs=[VM] * 2,
        out_specs=VM,
        compiler_params=pltpu.CompilerParams(vmem_limit_bytes=VMEM),
        cost_estimate=pl.CostEstimate(flops=8 * pad * 2048 * width, bytes_accessed=5 * 2**20, transcendentals=0),
        name="half",
    )(blocks, kt)


def sigma_kernel(scale, rows, place, h, near0, near1, far0, far1, out, buf, sem):
    yl, c = place[1], place[2]
    pairs = []
    for i, x in enumerate((near0, near1, far0, far1)):
        pairs += [(x.at[pl.ds(4 * k, 4)], buf.at[i, k]) for k in range(2)]
    copies = fetch(pairs, sem)
    pad, width = h.shape[1:]
    acc = None
    for i in range(4):
        for k in range(2):
            at = 4 * (2 * (yl if i % 2 == 0 else 1 - yl) + k) + 2 * (c if i < 2 else 1 - c)
            a = jnp.concatenate([h[at], h[at + 1]], axis=1)
            copies[2 * i + k].wait()
            term = dot(a, buf[i, k].reshape(-1, 2 * width), 1, 1)
            acc = term if acc is None else acc + term
    acc = acc * scale
    acc = jnp.concatenate([acc[:, b * pad : b * pad + rows] for b in range(acc.shape[1] // pad)], axis=1)
    out[...] = acc.astype(BF)


def sigma_call(place, h, near, far, rows, scale):
    pad = h.shape[1]
    width = near[0].shape[3]
    return pl.pallas_call(
        functools.partial(sigma_kernel, scale, rows),
        out_shape=jax.ShapeDtypeStruct((pad, 8 * rows), BF),
        in_specs=[SMEM, VM] + [ANY] * 4,
        out_specs=VM,
        scratch_shapes=[pltpu.VMEM((4, 2, 4, 2, pad, width), BF), pltpu.SemaphoreType.DMA((8,))],
        compiler_params=pltpu.CompilerParams(vmem_limit_bytes=VMEM),
        cost_estimate=pl.CostEstimate(flops=128 * pad * pad * width, bytes_accessed=8 * 2**20, transcendentals=0),
        name="sigma",
    )(place, h, *near, *far)


def local(green, colloc, core):
    nx = lax.axis_size("orb")
    c, x, tau, yl, z = (lax.axis_index(a) for a in ("c", "orb", "tau", "yl", "z"))
    place = jnp.stack([x, yl, c, z, yl]).astype(jnp.int32)
    rows, cols = colloc.shape
    pad = 192
    deep = pad + core.shape[0]
    half_cols = cols // 2
    quarter = cols // 4

    xpad = jnp.pad(colloc, ((0, pad - rows), (0, 0)))
    same, cross = [], []
    for i in range(32):
        for o in range(nx):
            to = o * 8 + i % 8
            same.append((i * nx + o, to * nx + i // 8))
            cross.append((i * nx + o, (to ^ 1) * nx + i // 8))

    def halves(value):
        low, high = value[:, :half_cols], value[:, half_cols:]
        return jnp.where(c == 0, low, high), jnp.where(c == 0, high, low)

    stay, go = halves(xpad)
    stay = lax.ppermute(stay, GRID + ("orb",), same)
    go = lax.ppermute(go, GRID + ("orb",), cross)
    zstay, zgo = halves(core)
    zgo = shift(zgo, "c", 1)
    stay, go = jnp.concatenate([stay, zstay]), jnp.concatenate([go, zgo])
    own = jnp.where(c == 0, jnp.stack([stay, go]), jnp.stack([go, stay]))

    tile = green[0]
    blocks = tile.shape[1] // rows
    g_own = jnp.pad(tile.reshape(rows, blocks, rows), ((0, pad - rows), (0, 0), (0, pad - rows)))
    g_own = g_own.reshape(pad, blocks * pad)
    own, g_own = lax.optimization_barrier((own, g_own))
    g_other = shift(g_own, "c", 1)

    one_way, other_way = [(0, 2), (2, 0), (1, 3), (3, 1)], [(0, 3), (3, 0), (1, 2), (2, 1)]

    def across(value, way):
        return lax.ppermute(value, ("yl", "tau"), way)

    up, down, mate_up, mate_down = [own], [own], [], []
    for d in range(4):
        moved = [shift(up[d], "z", 1), across(up[d], one_way)]
        if d > 0:
            moved.append(across(down[d], other_way))
        if d < 3:
            moved.append(shift(down[d], "z", -1))
        moved = lax.optimization_barrier(moved)
        up.append(moved[0])
        mate_up.append(moved[1])
        if d > 0:
            mate_down.append(moved[2])
        if d < 3:
            down.append(moved[-1])
    mate_up.append(across(up[4], other_way))
    ring, mate = up + down[1:], mate_up + mate_down

    tall = jnp.concatenate([xpad, core])
    tall, _ = lax.optimization_barrier((tall, up[2]))
    tall = lax.all_gather(tall, ("orb", "yl", "c"), axis=0, tiled=False)
    tall = tall.reshape(nx, 4, deep, cols)

    inner, zfirst, near0 = inner_call(place, g_own, g_other, ring)
    turned = jnp.stack([x, 1 - yl, c, z, yl]).astype(jnp.int32)
    inner, zsecond, near1 = inner_call(turned, g_own, g_other, mate, inner)
    zcols = jnp.where(yl == 0, jnp.stack([zfirst, zsecond]), jnp.stack([zsecond, zfirst]))
    zcols = zcols.reshape(nx * cols, quarter)
    near = [near0, near1]
    far = [shift(v, "c", 1) for v in near]

    inner = swap(inner.reshape(8, 2, pad, quarter), ("orb", "yl")).reshape(nx, 2, 2, pad, quarter)
    inner = jnp.sum(inner.astype(F32), axis=0).astype(BF)
    inner = jnp.where(c == 0, inner, inner[:, ::-1])
    inner = jnp.pad(inner, ((0, 0), (0, 0), (0, deep - pad), (0, 0))).reshape(4 * deep, quarter)

    stack = tall.reshape(nx, 4 * deep, cols)
    part = lax.dot_general(stack, inner, (((1,), (0,)), ((), ())), preferred_element_type=F32)
    part = part.astype(BF).reshape(16, quarter, quarter)
    got = swap(part, ("tau", "z"))
    g = jnp.sum(got.reshape(2, 8, quarter, quarter).astype(F32), axis=1).astype(BF)
    gf = g.astype(F32)
    pair = (gf[0] * gf[1]).astype(BF)
    prow = spread(pair, ("orb", "c", "yl"))
    prow = jnp.transpose(prow, (1, 0, 2)).reshape(quarter, 16 * quarter)
    left = dot(prow, zcols, 1, 0).astype(BF)
    left = spread(left, ("tau", "z")).reshape(16 * quarter, quarter)
    zr = lax.dynamic_slice_in_dim(tall[:, :, pad:], 2 * tau, 2, 1)
    zr = jnp.transpose(zr, (1, 2, 0, 3)).reshape(quarter, nx * cols)
    screened = dot(zr, left, 1, 0)
    kern = (gf * screened[None]).astype(BF)
    kt = jnp.broadcast_to(kern[:, None], (2, 8, quarter, quarter)).reshape(16, quarter, quarter)
    kt = swap(kt, ("tau", "z")).reshape(nx, cols, quarter)
    half = half_call(tall, kt, pad)
    half = jnp.broadcast_to(half[None], (nx, 4, pad, quarter))
    hrow = swap(half.reshape(16, pad, quarter), ("orb", "c", "yl"))
    return sigma_call(place, hrow, near, far, rows, -1.0 / (nx * cols))[None, :rows]


def solution(mesh):
    fine = Mesh(mesh.devices.reshape(2, 8, 2, 4, 2), GRID + ("orb", "tau"))
    placed = (P("tau", GRID, "orb"), P(GRID, "orb"), P(GRID, "orb"))
    return jax.shard_map(
        local, mesh=fine, in_specs=placed, out_specs=P("tau", GRID, "orb"), check_vma=False
    )
```

time: 307 us -> 233 us (0.76)
  blocking collectives: 118 us -> 32.6 us
  starting transfers between devices: 45.2 us -> 77.7 us
  matrix products: 24.8 us -> 4.17 us
  Pallas kernels: 0 us -> 20 us
  waiting for transfers between devices: 81.6 us -> 64 us
    all_to_all x4 -> x2, blocking collectives: 77.7 us -> 32.6 us  [swap(): return lax.all_to_all(value, axes, 0, 0, tiled=True)]
    all_gather x2 -> x0, blocking collectives: 40.7 us -> none  [the longest x1 32.4 us: local(): zr = lax.all_gather(zr, 'orb', axis=1, tiled=True)]
    ppermute x8 -> x11, waiting for transfers between devices: 32.7 us -> 7.2 us  [shift(): return lax.ppermute(value, axis, [(i, (i + by) % n) for i in range(n)])]
    ppermute x0 -> x10, starting transfers between devices: none -> 22.1 us  [the longest x8 18.1 us: across(): return lax.ppermute(value, ('yl', 'tau'), way)]
    dot_general x22 -> x2, matrix products: 21.9 us -> 0.62 us  [dot(): lax.dot_general(a, b, (((ca,), (cb,)), ((), ())), preferred_element_type=...]
    pallas_call x0 -> x4, Pallas kernels: none -> 20 us  [the longest x2 10.1 us: inner_call(): pl.pallas_call(functools.partial(inner_kernel, second), out_shape=(jax.Sh...]
    ppermute x8 -> x11, starting transfers between devices: 14.2 us -> 23.1 us  [shift(): return lax.ppermute(value, axis, [(i, (i + by) % n) for i in range(n)])]
    ppermute x0 -> x10, waiting for transfers between devices: none -> 4.01 us  [the longest x8 4 us: across(): return lax.ppermute(value, ('yl', 'tau'), way)]
  transfers between devices with their start and end apart: 15 -> 26, of which waited for: 7 -> 12; matrix products, arithmetic and copies ran while one was open for 11% -> 4% of each run, Pallas kernels for 0% -> 6%
where the time goes in v2:
time: 233 us; the launch traced here: 232 us
  starting transfers between devices  77.7 us (33%)
  waiting for transfers between devices  64 us (27%)
  blocking collectives  32.6 us (14%)
  Pallas kernels  20 us (9%)
  local copies, waits for them, and re-layouts  16.6 us (7%)
  between operations  13.9 us (6%)
  matrix products  4.17 us (2%)
  other arithmetic  3.07 us (1%)
    all_to_all x4, waiting for transfers between devices, swap(): return lax.all_to_all(value, axes, 0, 0, tiled=True)  52.8 us
    all_to_all x2, blocking collectives, swap(): return lax.all_to_all(value, axes, 0, 0, tiled=True)  32.6 us
    all_to_all x4, starting transfers between devices, swap(): return lax.all_to_all(value, axes, 0, 0, tiled=True)  32.5 us
    ppermute x11, starting transfers between devices, shift(): return lax.ppermute(value, axis, [(i, (i + by) % n) for i in range(n)])  23.1 us
    ppermute x8, starting transfers between devices, across(): return lax.ppermute(value, ('yl', 'tau'), way)  18.1 us
    pallas_call x2, Pallas kernels, inner_call(): pl.pallas_call(functools.partial(inner_kernel, second), out_shape=(jax.Sh...  10.1 us
    ppermute x11, waiting for transfers between devices, shift(): return lax.ppermute(value, axis, [(i, (i + by) % n) for i in range(n)])  7.2 us
    pallas_call x1, Pallas kernels, sigma_call(): pl.pallas_call(functools.partial(sigma_kernel, scale, rows), out_shape=ja...  5.98 us
  transfers between devices with their start and end apart: 26, of which 12 were waited for; matrix products, arithmetic and copies ran while one was open for 4% of the time, Pallas kernels for 6%

profile of v2, /device:TPU:1, one launch (start us, length us, event | category | flops | bytes accessed | tf_op | source)
XLA Modules:
  0.0 232.0 jit_solution(17621294199553006577)
XLA Ops:
  7.7 3.3 %collective-permute-start.1 = (bf16[192,256]{1,0:T(8,128)(2,1)S(1)}, bf16[192,256]{1,0:T(8,128)(2,1)S(1)}, u32[]{:S(2)}, u32[]{:S(2)}) collective-permute-start(bf16[192,256]{1,0:T(8,128)(2,1)S(1)} %get-tuple-element.52), channel_id=1, source_target_pairs={{0,8},{2,72},{4,136},{6,200},{8,0},{10,64},{12,128},{14,192},{16,2... | collective-permute-start | bytes 294920 | tf_op jit(solution)/shard_map/ppermute | solution.py:184
  12.6 2.3 %reshape_squeeze.3 = bf16[188,8,188]{2,1,0:T(8,128)(2,1)S(1)} reshape(bf16[1,188,1504]{2,1,0:T(8,128)(2,1)} %param.3) | data formatting | bytes 1131008 | tf_op jit(solution)/shard_map/reshape;squeeze | solution.py:192
  15.9 8.0 %collective-permute-start.4 = (bf16[2,256,256]{2,1,0:T(8,128)(2,1)S(1)}, bf16[2,256,256]{2,1,0:T(8,128)(2,1)S(1)}, u32[]{:S(2)}, u32[]{:S(2)}) collective-permute-start(bf16[2,256,256]{2,1,0:T(8,128)(2,1)S(1)} %maximum_select_fusion.1.refs_0_), channel_id=1, source_target_pairs={{0,128},{128,0},{1,129},{129,1},{2,130},{130,2},{3,131},{131,3},{4... | collective-permute-start | bytes 786440 | tf_op jit(solution)/shard_map/ppermute | solution.py:200
  23.9 9.2 %collective-permute-start.5 = (bf16[2,256,256]{2,1,0:T(8,128)(2,1)S(1)}, bf16[2,256,256]{2,1,0:T(8,128)(2,1)S(1)}, u32[]{:S(2)}, u32[]{:S(2)}) collective-permute-start(bf16[2,256,256]{2,1,0:T(8,128)(2,1)S(1)} %maximum_select_fusion.1.refs_0_), channel_id=1, source_target_pairs={{0,112},{16,0},{32,16},{48,32},{64,48},{80,64},{96,80},{112,96},{1... | collective-permute-start | bytes 786440 | tf_op jit(solution)/shard_map/ppermute | solution.py:28
  33.6 3.4 %collective-permute-done.5.refs_5_ = bf16[2,256,256]{2,1,0:T(8,128)(2,1)S(1)} collective-permute-done((bf16[2,256,256]{2,1,0:T(8,128)(2,1)S(1)}, bf16[2,256,256]{2,1,0:T(8,128)(2,1)S(1)}, u32[]{:S(2)}, u32[]{:S(2)}) %collective-permute-start.5) | collective-permute-done | bytes 262176 | tf_op jit(solution)/shard_map/ppermute | solution.py:28
  40.3 3.4 %collective-permute-start.9 = (bf16[2,256,256]{2,1,0:T(8,128)(2,1)S(1)}, bf16[2,256,256]{2,1,0:T(8,128)(2,1)}, u32[]{:S(2)}, u32[]{:S(2)}) collective-permute-start(bf16[2,256,256]{2,1,0:T(8,128)(2,1)S(1)} %collective-permute-done.5.refs_5_), channel_id=1, source_target_pairs={{0,112},{16,0},{32,16},{48,32},{64,48},{80,64},{96,80},{112,96},{1... | collective-permute-start | bytes 786440 | tf_op jit(solution)/shard_map/ppermute | solution.py:28
  48.7 2.3 collective-permute-start.14
  51.0 4.9 %collective-permute-start.10 = (bf16[192,1536]{1,0:T(8,128)(2,1)S(1)}, bf16[192,1536]{1,0:T(8,128)(2,1)S(1)}, u32[]{:S(2)}, u32[]{:S(2)}) collective-permute-start(bf16[192,1536]{1,0:T(8,128)(2,1)S(1)} %reshape.60.own), channel_id=1, source_target_pairs={{0,8},{8,0},{1,9},{9,1},{2,10},{10,2},{3,11},{11,3},{4,12},{12,4},... | collective-permute-start | bytes 1769480 | tf_op jit(solution)/shard_map/ppermute | solution.py:28
  63.1 2.8 %collective-permute-done.17.refs_7_ = bf16[2,256,256]{2,1,0:T(8,128)(2,1)S(1)} collective-permute-done((bf16[2,256,256]{2,1,0:T(8,128)(2,1)S(1)}, bf16[2,256,256]{2,1,0:T(8,128)(2,1)S(1)}, u32[]{:S(2)}, u32[]{:S(2)}) %collective-permute-start.17) | collective-permute-done | bytes 262176 | tf_op jit(solution)/shard_map/ppermute | solution.py:200
  71.0 4.9 %inner.2 = (bf16[2,2,2,192,128]{4,3,2,1,0:T(8,128)(2,1)}, bf16[1024,128]{1,0:T(8,128)(2,1)}, bf16[8,2,192,256]{3,2,1,0:T(8,128)(2,1)}) custom-call(s32[5]{0:T(128)} %stack.58.place, bf16[192,1536]{1,0:T(8,128)(2,1)} %copy-done, bf16[192,1536]{1,0:T(8,128)(2,1)} %copy-done.2, bf16[2,256,256]{2,1,0:T(8,128)(2,1)} %copy-done.5, ...), custom_call_target="tpu_custom_call" | custom-call | flops 603979776 | bytes 6291456 | tf_op jit(solution)/shard_map/inner/pallas_call | solution.py:92
  76.0 5.1 %inner.3 = (bf16[4,2,2,192,128]{4,3,2,1,0:T(8,128)(2,1)}, bf16[1024,128]{1,0:T(8,128)(2,1)}, bf16[8,2,192,256]{3,2,1,0:T(8,128)(2,1)}) custom-call(s32[5]{0:T(128)} %stack.64.place, bf16[192,1536]{1,0:T(8,128)(2,1)} %copy-done, bf16[192,1536]{1,0:T(8,128)(2,1)} %copy-done.2, bf16[2,256,256]{2,1,0:T(8,128)(2,1)} %copy-done.10, ...), custom_call_target="tpu_custom_call" | custom-call | flops 603979776 | bytes 6291456 | tf_op jit(solution)/shard_map/inner/pallas_call | solution.py:92
  81.1 16.0 %all_to_all.30 = bf16[8,2,192,128]{3,2,1,0:T(8,128)(2,1)S(1)} all-to-all(bf16[8,2,192,128]{3,2,1,0:T(8,128)(2,1)} %bitcast.54), channel_id=1, replica_groups=mesh['yl'=2,'z'=8,'c'=2,'orb'=4,'tau'=2] {'orb','yl'}, dimensions={0} | all-to-all | bytes 1572864 | tf_op jit(solution)/shard_map/all_to_all | solution.py:18
  97.4 3.5 %convolution_convert_fusion = bf16[4,512,128]{2,1,0:T(8,128)(2,1)S(1)} fusion(bf16[4,1024,512]{2,1,0:T(8,128)(2,1)} %bitcast.44, bf16[1024,128,1]{1,0,2:T(8,128)(2,1)S(1)} %bitcast.56), kind=kOutput, calls=%fused_computation | convolution fusion | flops 537133056 | bytes 4980736 | tf_op jit(solution)/shard_map/dot_general | solution.py:238
  101.0 16.6 %all_to_all.31 = bf16[16,128,128]{2,1,0:T(8,128)(2,1)S(1)} all-to-all(bf16[16,128,128]{2,1,0:T(8,128)(2,1)S(1)} %bitcast.55), channel_id=1, replica_groups=mesh['yl'=2,'z'=8,'c'=2,'orb'=4,'tau'=2] {'tau','z'}, dimensions={0} | all-to-all | bytes 1048576 | tf_op jit(solution)/shard_map/all_to_all | solution.py:18
  118.7 15.2 %all-to-all-start.2 = ((bf16[16,128,128]{1,2,0:T(8,128)(2,1)}), bf16[16,128,128]{1,2,0:T(8,128)(2,1)S(1)}, u32[]{:S(2)}, u32[]{:S(2)}) async-start(bf16[16,128,128]{1,2,0:T(8,128)(2,1)} %broadcast_in_dim.13), calls=%async_computation.2 | async-start | bytes 1048576 | tf_op jit(solution)/shard_map/all_to_all | solution.py:18
  134.0 11.0 %all-to-all-done.2 = bf16[16,128,128]{1,2,0:T(8,128)(2,1)S(1)} async-done(((bf16[16,128,128]{1,2,0:T(8,128)(2,1)}), bf16[16,128,128]{1,2,0:T(8,128)(2,1)S(1)}, u32[]{:S(2)}, u32[]{:S(2)}) %all-to-all-start.2) | async-done | bytes 524320 | tf_op jit(solution)/shard_map/all_to_all | solution.py:18
  146.2 4.3 %all-to-all-start.3 = ((bf16[16,128,128]{2,1,0:T(8,128)(2,1)}), bf16[16,128,128]{2,1,0:T(8,128)(2,1)S(1)}, u32[]{:S(2)}, u32[]{:S(2)}) async-start(bf16[16,128,128]{2,1,0:T(8,128)(2,1)} %broadcast_in_dim.14), calls=%async_computation.3 | async-start | bytes 1048576 | tf_op jit(solution)/shard_map/all_to_all | solution.py:18
  152.6 13.1 %all-to-all-done.3 = bf16[16,128,128]{2,1,0:T(8,128)(2,1)S(1)} async-done(((bf16[16,128,128]{2,1,0:T(8,128)(2,1)}), bf16[16,128,128]{2,1,0:T(8,128)(2,1)S(1)}, u32[]{:S(2)}, u32[]{:S(2)}) %all-to-all-start.3) | async-done | bytes 524320 | tf_op jit(solution)/shard_map/all_to_all | solution.py:18
  166.9 6.7 %all-to-all-start.4 = ((bf16[16,128,128]{2,1,0:T(8,128)(2,1)}), bf16[16,128,128]{2,1,0:T(8,128)(2,1)S(1)}, u32[]{:S(2)}, u32[]{:S(2)}) async-start(bf16[16,128,128]{2,1,0:T(8,128)(2,1)} %bitcast.23), calls=%async_computation.4 | async-start | bytes 1048576 | tf_op jit(solution)/shard_map/all_to_all | solution.py:18
  174.6 14.1 %all-to-all-done.4 = bf16[16,128,128]{2,1,0:T(8,128)(2,1)S(1)} async-done(((bf16[16,128,128]{2,1,0:T(8,128)(2,1)}), bf16[16,128,128]{2,1,0:T(8,128)(2,1)S(1)}, u32[]{:S(2)}, u32[]{:S(2)}) %all-to-all-start.4) | async-done | bytes 524320 | tf_op jit(solution)/shard_map/all_to_all | solution.py:18
  189.5 3.9 %half.1 = bf16[4,192,128]{2,1,0:T(8,128)(2,1)} custom-call(bf16[4,4,256,512]{3,2,1,0:T(8,128)(2,1)} %bitcast.46, bf16[4,512,128]{2,1,0:T(8,128)(2,1)} %bitcast.48), custom_call_target="tpu_custom_call" | custom-call | flops 402653184 | bytes 5242880 | tf_op jit(solution)/shard_map/half/pallas_call | solution.py:114
  195.4 6.3 %all-to-all-start.5 = ((bf16[16,192,128]{2,1,0:T(8,128)(2,1)}), bf16[16,192,128]{2,1,0:T(8,128)(2,1)S(1)}, u32[]{:S(2)}, u32[]{:S(2)}) async-start(bf16[16,192,128]{2,1,0:T(8,128)(2,1)} %bitcast.25), calls=%async_computation.5 | async-start | bytes 1572864 | tf_op jit(solution)/shard_map/all_to_all | solution.py:18
  201.7 14.7 %all-to-all-done.5.h = bf16[16,192,128]{2,1,0:T(8,128)(2,1)S(1)} async-done(((bf16[16,192,128]{2,1,0:T(8,128)(2,1)}), bf16[16,192,128]{2,1,0:T(8,128)(2,1)S(1)}, u32[]{:S(2)}, u32[]{:S(2)}) %all-to-all-start.5) | async-done | bytes 786464 | tf_op jit(solution)/shard_map/all_to_all | solution.py:18
  217.2 6.0 %sigma.1 = bf16[192,1504]{1,0:T(8,128)(2,1)} custom-call(s32[5]{0:T(128)} %stack.58.place, bf16[16,192,128]{2,1,0:T(8,128)(2,1)} %copy-done.1, bf16[8,2,192,256]{3,2,1,0:T(8,128)(2,1)} %get-tuple-element.49.near0, bf16[8,2,192,256]{3,2,1,0:T(8,128)(2,1)} %get-tuple-element.50.near1, bf16[8,2,192,256]{3,2,1,0:T(8,128)(2,1)} %collective-permute-done.19.far0, ...), custom_call_target="tpu_custom_call" | custom-call | flops 1207959552 | bytes 8388608 | tf_op jit(solution)/shard_map/sigma/pallas_call | solution.py:148
  (110 shorter events, 37.3 us)
Async XLA Ops:
  6.5 90.8 %all-gather.3.cloned.1.call-start = ((), (), s32[]{:S(2)}) async-start(), calls=%async_computation.6 | async-start | bytes 4456448 | tf_op jit(solution)/shard_map/all_gather | solution.py:221
  7.7 8.1 %collective-permute-start.1 = (bf16[192,256]{1,0:T(8,128)(2,1)S(1)}, bf16[192,256]{1,0:T(8,128)(2,1)S(1)}, u32[]{:S(2)}, u32[]{:S(2)}) collective-permute-start(bf16[192,256]{1,0:T(8,128)(2,1)S(1)} %get-tuple-element.52), channel_id=1, source_target_pairs={{0,8},{2,72},{4,136},{6,200},{8,0},{10,64},{12,128},{14,192},{16,2... | collective-permute-start | bytes 294920 | tf_op jit(solution)/shard_map/ppermute | solution.py:184
  15.9 17.8 %collective-permute-start.3 = (bf16[2,256,256]{2,1,0:T(8,128)(2,1)S(1)}, bf16[2,256,256]{2,1,0:T(8,128)(2,1)S(1)}, u32[]{:S(2)}, u32[]{:S(2)}) collective-permute-start(bf16[2,256,256]{2,1,0:T(8,128)(2,1)S(1)} %maximum_select_fusion.1.refs_0_), channel_id=1, source_target_pairs={{0,16},{16,32},{32,48},{48,64},{64,80},{80,96},{96,112},{112,0},{1... | collective-permute-start | bytes 786440 | tf_op jit(solution)/shard_map/ppermute | solution.py:28
  15.9 17.7 %collective-permute-start.4 = (bf16[2,256,256]{2,1,0:T(8,128)(2,1)S(1)}, bf16[2,256,256]{2,1,0:T(8,128)(2,1)S(1)}, u32[]{:S(2)}, u32[]{:S(2)}) collective-permute-start(bf16[2,256,256]{2,1,0:T(8,128)(2,1)S(1)} %maximum_select_fusion.1.refs_0_), channel_id=1, source_target_pairs={{0,128},{128,0},{1,129},{129,1},{2,130},{130,2},{3,131},{131,3},{4... | collective-permute-start | bytes 786440 | tf_op jit(solution)/shard_map/ppermute | solution.py:200
  23.9 13.1 %collective-permute-start.5 = (bf16[2,256,256]{2,1,0:T(8,128)(2,1)S(1)}, bf16[2,256,256]{2,1,0:T(8,128)(2,1)S(1)}, u32[]{:S(2)}, u32[]{:S(2)}) collective-permute-start(bf16[2,256,256]{2,1,0:T(8,128)(2,1)S(1)} %maximum_select_fusion.1.refs_0_), channel_id=1, source_target_pairs={{0,112},{16,0},{32,16},{48,32},{64,48},{80,64},{96,80},{112,96},{1... | collective-permute-start | bytes 786440 | tf_op jit(solution)/shard_map/ppermute | solution.py:28
  37.0 7.5 %collective-permute-start.6 = (bf16[2,256,256]{2,1,0:T(8,128)(2,1)S(1)}, bf16[2,256,256]{2,1,0:T(8,128)(2,1)S(1)}, u32[]{:S(2)}, u32[]{:S(2)}) collective-permute-start(bf16[2,256,256]{2,1,0:T(8,128)(2,1)S(1)} %collective-permute-done.3.refs_1_), channel_id=1, source_target_pairs={{0,16},{16,32},{32,48},{48,64},{64,80},{80,96},{96,112},{112,0},{1... | collective-permute-start | bytes 786440 | tf_op jit(solution)/shard_map/ppermute | solution.py:28
  37.1 7.5 %collective-permute-start.7 = (bf16[2,256,256]{2,1,0:T(8,128)(2,1)S(1)}, bf16[2,256,256]{2,1,0:T(8,128)(2,1)S(1)}, u32[]{:S(2)}, u32[]{:S(2)}) collective-permute-start(bf16[2,256,256]{2,1,0:T(8,128)(2,1)S(1)} %collective-permute-done.3.refs_1_), channel_id=1, source_target_pairs={{0,128},{128,0},{1,129},{129,1},{2,130},{130,2},{3,131},{131,3},{4... | collective-permute-start | bytes 786440 | tf_op jit(solution)/shard_map/ppermute | solution.py:200
  38.4 6.8 %collective-permute-start.8 = (bf16[2,256,256]{2,1,0:T(8,128)(2,1)S(1)}, bf16[2,256,256]{2,1,0:T(8,128)(2,1)S(1)}, u32[]{:S(2)}, u32[]{:S(2)}) collective-permute-start(bf16[2,256,256]{2,1,0:T(8,128)(2,1)S(1)} %collective-permute-done.5.refs_5_), channel_id=1, source_target_pairs={{0,129},{129,0},{1,128},{128,1},{2,131},{131,2},{3,130},{130,3},{4... | collective-permute-start | bytes 786440 | tf_op jit(solution)/shard_map/ppermute | solution.py:200
  40.3 6.7 %collective-permute-start.9 = (bf16[2,256,256]{2,1,0:T(8,128)(2,1)S(1)}, bf16[2,256,256]{2,1,0:T(8,128)(2,1)}, u32[]{:S(2)}, u32[]{:S(2)}) collective-permute-start(bf16[2,256,256]{2,1,0:T(8,128)(2,1)S(1)} %collective-permute-done.5.refs_5_), channel_id=1, source_target_pairs={{0,112},{16,0},{32,16},{48,32},{64,48},{80,64},{96,80},{112,96},{1... | collective-permute-start | bytes 786440 | tf_op jit(solution)/shard_map/ppermute | solution.py:28
  47.0 8.8 %collective-permute-start.11 = (bf16[2,256,256]{2,1,0:T(8,128)(2,1)S(1)}, bf16[2,256,256]{2,1,0:T(8,128)(2,1)S(1)}, u32[]{:S(2)}, u32[]{:S(2)}) collective-permute-start(bf16[2,256,256]{2,1,0:T(8,128)(2,1)S(1)} %collective-permute-done.6.refs_2_), channel_id=1, source_target_pairs={{0,16},{16,32},{32,48},{48,64},{64,80},{80,96},{96,112},{112,0},{1... | collective-permute-start | bytes 786440 | tf_op jit(solution)/shard_map/ppermute | solution.py:28
  47.4 8.4 %collective-permute-start.12 = (bf16[2,256,256]{2,1,0:T(8,128)(2,1)S(1)}, bf16[2,256,256]{2,1,0:T(8,128)(2,1)S(1)}, u32[]{:S(2)}, u32[]{:S(2)}) collective-permute-start(bf16[2,256,256]{2,1,0:T(8,128)(2,1)S(1)} %collective-permute-done.6.refs_2_), channel_id=1, source_target_pairs={{0,128},{128,0},{1,129},{129,1},{2,130},{130,2},{3,131},{131,3},{4... | collective-permute-start | bytes 786440 | tf_op jit(solution)/shard_map/ppermute | solution.py:200
  47.7 8.1 %collective-permute-start.13 = (bf16[2,256,256]{2,1,0:T(8,128)(2,1)}, bf16[2,256,256]{2,1,0:T(8,128)(2,1)}, u32[]{:S(2)}, u32[]{:S(2)}) collective-permute-start(bf16[2,256,256]{2,1,0:T(8,128)(2,1)} %collective-permute-done.9.refs_6_), channel_id=1, source_target_pairs={{0,129},{129,0},{1,128},{128,1},{2,131},{131,2},{3,130},{130,3},{4... | collective-permute-start | bytes 786440 | tf_op jit(solution)/shard_map/ppermute | solution.py:200
  48.7 7.2 %collective-permute-start.14 = (bf16[2,256,256]{2,1,0:T(8,128)(2,1)}, bf16[2,256,256]{2,1,0:T(8,128)(2,1)S(1)}, u32[]{:S(2)}, u32[]{:S(2)}) collective-permute-start(bf16[2,256,256]{2,1,0:T(8,128)(2,1)} %collective-permute-done.9.refs_6_), channel_id=1, source_target_pairs={{0,112},{16,0},{32,16},{48,32},{64,48},{80,64},{96,80},{112,96},{1... | collective-permute-start | bytes 786440 | tf_op jit(solution)/shard_map/ppermute | solution.py:28
  51.0 19.1 %collective-permute-start.10 = (bf16[192,1536]{1,0:T(8,128)(2,1)S(1)}, bf16[192,1536]{1,0:T(8,128)(2,1)S(1)}, u32[]{:S(2)}, u32[]{:S(2)}) collective-permute-start(bf16[192,1536]{1,0:T(8,128)(2,1)S(1)} %reshape.60.own), channel_id=1, source_target_pairs={{0,8},{8,0},{1,9},{9,1},{2,10},{10,2},{3,11},{11,3},{4,12},{12,4},... | collective-permute-start | bytes 1769480 | tf_op jit(solution)/shard_map/ppermute | solution.py:28
  55.9 6.6 %collective-permute-start.15 = (bf16[2,256,256]{2,1,0:T(8,128)(2,1)S(1)}, bf16[2,256,256]{2,1,0:T(8,128)(2,1)}, u32[]{:S(2)}, u32[]{:S(2)}) collective-permute-start(bf16[2,256,256]{2,1,0:T(8,128)(2,1)S(1)} %collective-permute-done.11.refs_3_), channel_id=1, source_target_pairs={{0,16},{16,32},{32,48},{48,64},{64,80},{80,96},{96,112},{112,0},{1... | collective-permute-start | bytes 786440 | tf_op jit(solution)/shard_map/ppermute | solution.py:28
  57.7 5.4 %collective-permute-start.16 = (bf16[2,256,256]{2,1,0:T(8,128)(2,1)S(1)}, bf16[2,256,256]{2,1,0:T(8,128)(2,1)S(1)}, u32[]{:S(2)}, u32[]{:S(2)}) collective-permute-start(bf16[2,256,256]{2,1,0:T(8,128)(2,1)S(1)} %collective-permute-done.11.refs_3_), channel_id=1, source_target_pairs={{0,128},{128,0},{1,129},{129,1},{2,130},{130,2},{3,131},{131,3},{4... | collective-permute-start | bytes 786440 | tf_op jit(solution)/shard_map/ppermute | solution.py:200
  59.0 6.8 %collective-permute-start.17 = (bf16[2,256,256]{2,1,0:T(8,128)(2,1)S(1)}, bf16[2,256,256]{2,1,0:T(8,128)(2,1)S(1)}, u32[]{:S(2)}, u32[]{:S(2)}) collective-permute-start(bf16[2,256,256]{2,1,0:T(8,128)(2,1)S(1)} %collective-permute-done.14.refs_7_), channel_id=1, source_target_pairs={{0,129},{129,0},{1,128},{128,1},{2,131},{131,2},{3,130},{130,3},{4... | collective-permute-start | bytes 786440 | tf_op jit(solution)/shard_map/ppermute | solution.py:200
  66.5 9.4 %collective-permute-start.18 = (bf16[2,256,256]{2,1,0:T(8,128)(2,1)}, bf16[2,256,256]{2,1,0:T(8,128)(2,1)}, u32[]{:S(2)}, u32[]{:S(2)}) collective-permute-start(bf16[2,256,256]{2,1,0:T(8,128)(2,1)} %collective-permute-done.15.refs_4_), channel_id=1, source_target_pairs={{0,129},{129,0},{1,128},{128,1},{2,131},{131,2},{3,130},{130,3},{4... | collective-permute-start | bytes 786440 | tf_op jit(solution)/shard_map/ppermute | solution.py:200
  118.7 26.3 %all-to-all-start.2 = ((bf16[16,128,128]{1,2,0:T(8,128)(2,1)}), bf16[16,128,128]{1,2,0:T(8,128)(2,1)S(1)}, u32[]{:S(2)}, u32[]{:S(2)}) async-start(bf16[16,128,128]{1,2,0:T(8,128)(2,1)} %broadcast_in_dim.13), calls=%async_computation.2 | async-start | bytes 1048576 | tf_op jit(solution)/shard_map/all_to_all | solution.py:18
  146.2 19.5 %all-to-all-start.3 = ((bf16[16,128,128]{2,1,0:T(8,128)(2,1)}), bf16[16,128,128]{2,1,0:T(8,128)(2,1)S(1)}, u32[]{:S(2)}, u32[]{:S(2)}) async-start(bf16[16,128,128]{2,1,0:T(8,128)(2,1)} %broadcast_in_dim.14), calls=%async_computation.3 | async-start | bytes 1048576 | tf_op jit(solution)/shard_map/all_to_all | solution.py:18
  166.9 21.9 %all-to-all-start.4 = ((bf16[16,128,128]{2,1,0:T(8,128)(2,1)}), bf16[16,128,128]{2,1,0:T(8,128)(2,1)S(1)}, u32[]{:S(2)}, u32[]{:S(2)}) async-start(bf16[16,128,128]{2,1,0:T(8,128)(2,1)} %bitcast.23), calls=%async_computation.4 | async-start | bytes 1048576 | tf_op jit(solution)/shard_map/all_to_all | solution.py:18
  173.6 28.1 %collective-permute-start.19 = (bf16[8,2,192,256]{3,2,1,0:T(8,128)(2,1)S(1)}, bf16[8,2,192,256]{3,2,1,0:T(8,128)(2,1)}, u32[]{:S(2)}, u32[]{:S(2)}) collective-permute-start(bf16[8,2,192,256]{3,2,1,0:T(8,128)(2,1)S(1)} %copy-done.4), channel_id=1, source_target_pairs={{0,8},{8,0},{1,9},{9,1},{2,10},{10,2},{3,11},{11,3},{4,12},{12,4},... | collective-permute-start | bytes 4718600 | tf_op jit(solution)/shard_map/ppermute | solution.py:28
  174.5 27.2 %collective-permute-start.20 = (bf16[8,2,192,256]{3,2,1,0:T(8,128)(2,1)}, bf16[8,2,192,256]{3,2,1,0:T(8,128)(2,1)}, u32[]{:S(2)}, u32[]{:S(2)}) collective-permute-start(bf16[8,2,192,256]{3,2,1,0:T(8,128)(2,1)} %get-tuple-element.50.near1), channel_id=1, source_target_pairs={{0,8},{8,0},{1,9},{9,1},{2,10},{10,2},{3,11},{11,3},{4,12},{12,4},... | collective-permute-start | bytes 4718600 | tf_op jit(solution)/shard_map/ppermute | solution.py:28
  195.4 20.9 %all-to-all-start.5 = ((bf16[16,192,128]{2,1,0:T(8,128)(2,1)}), bf16[16,192,128]{2,1,0:T(8,128)(2,1)S(1)}, u32[]{:S(2)}, u32[]{:S(2)}) async-start(bf16[16,192,128]{2,1,0:T(8,128)(2,1)} %bitcast.25), calls=%async_computation.5 | async-start | bytes 1572864 | tf_op jit(solution)/shard_map/all_to_all | solution.py:18
  (23 other events, 521.6 us)
Sparse Core Ops, SparseCore 0:
  47.1 46.2 all-gather.2

commit v3 on v2

--- a/solution.py
+++ b/solution.py
@@ -43,16 +43,21 @@
     return [z] + [lax.rem(z - d + n, n) for d in (1, 2, 3, 4)] + [lax.rem(z + d, n) for d in (1, 2, 3)]
 
 
-def inner_kernel(second, place, own, other, *refs):
+def slot_of(p, x):
+    return jnp.where(lax.div(p, 4) == lax.rem(x, 2), p, 4 * lax.div(p, 4) + 3 - lax.rem(p, 4))
+
+
+def inner_kernel(second, own, other, *refs):
     ring, refs = refs[:8], refs[8:]
     if second:
         before, refs = refs[0], refs[1:]
     out, zc, rows_out, xbuf, xsem, osem = refs
-    yl, z = place[1], place[3]
-    copies = fetch([(r, xbuf.at[p]) for r, p in zip(ring, ring_places(z, 8))], xsem)
+    x, yl, z = (lax.axis_index(a) for a in ("orb", "yl", "z"))
+    of = 1 - yl if second else yl
+    copies = fetch([(r, xbuf.at[slot_of(p, x)]) for r, p in zip(ring, ring_places(z, 8))], xsem)
     if second:
         for k in range(2):
-            out[2 * (1 - yl) + k] = before[k]
+            out[2 * yl + k] = before[k]
     for copy in copies:
         copy.wait()
     rows, width = own.shape[0], out.shape[4]
@@ -63,9 +68,11 @@
         for side, block in enumerate((own, other)):
             term = dot(block[...], panel, 1, 0).astype(BF)
             for part in range(2):
-                out[2 * yl + k if second else k, part, side] = term[:, part * width : (part + 1) * width]
-    cols = pl.ds(pl.multiple_of(place[4] * width, width), width)
-    zc[...] = xbuf[:, :, rows:, cols].reshape(zc.shape)
+                out[2 * of + k if second else k, part, side] = term[:, part * width : (part + 1) * width]
+    cols = pl.ds(pl.multiple_of(yl * width, width), width)
+    strip = zc.shape[0] // 8
+    for p in range(8):
+        zc[p * strip : (p + 1) * strip] = xbuf[slot_of(p, x), :, rows:, cols].reshape(strip, width)
     store.wait()
 
 
@@ -76,7 +83,8 @@
         for o in range(kt.shape[0]):
             term = dot(blocks[o, q, :pad], kt[o], 1, 0)
             acc = term if acc is None else acc + term
-        out[2 * (q % 2) + q // 2] = acc.astype(BF)
+        for o in range(kt.shape[0]):
+            out[4 * o + 2 * (q % 2) + q // 2] = acc.astype(BF)
 
 
 ANY = pl.BlockSpec(memory_space=pl.ANY)
@@ -84,7 +92,7 @@
 VM = pl.BlockSpec(memory_space=pltpu.VMEM)
 
 
-def inner_call(place, own, other, ring, before=None):
+def inner_call(own, other, ring, before=None):
     rows, k = own.shape
     deep, width = ring[0].shape[1:]
     second = before is not None
@@ -96,7 +104,7 @@
             jax.ShapeDtypeStruct((16 * (deep - rows), width // 2), BF),
             jax.ShapeDtypeStruct((8, 2, rows, width), BF),
         ),
-        in_specs=[SMEM, VM, VM] + [ANY] * 8 + [VM] * second,
+        in_specs=[VM, VM] + [VM] * 8 + [VM] * second,
         out_specs=(VM, VM, ANY),
         scratch_shapes=[
             pltpu.VMEM((8, 2, deep, width), BF),
@@ -106,14 +114,14 @@
         compiler_params=pltpu.CompilerParams(vmem_limit_bytes=VMEM),
         cost_estimate=pl.CostEstimate(flops=8 * rows * k * width, bytes_accessed=6 * 2**20, transcendentals=0),
         name="inner",
-    )(place, own, other, *ring, *([before] if second else []))
+    )(own, other, *ring, *([before] if second else []))
 
 
 def half_call(blocks, kt, pad):
     width = kt.shape[2]
     return pl.pallas_call(
         half_kernel,
-        out_shape=jax.ShapeDtypeStruct((4, pad, width), BF),
+        out_shape=jax.ShapeDtypeStruct((16, pad, width), BF),
         in_specs=[VM] * 2,
         out_specs=VM,
         compiler_params=pltpu.CompilerParams(vmem_limit_bytes=VMEM),
@@ -122,45 +130,38 @@
     )(blocks, kt)
 
 
-def sigma_kernel(scale, rows, place, h, near0, near1, far0, far1, out, buf, sem):
-    yl, c = place[1], place[2]
-    pairs = []
-    for i, x in enumerate((near0, near1, far0, far1)):
-        pairs += [(x.at[pl.ds(4 * k, 4)], buf.at[i, k]) for k in range(2)]
-    copies = fetch(pairs, sem)
+def sigma_kernel(scale, rows, h, near0, near1, far0, far1, out):
+    yl, c = lax.axis_index("yl"), lax.axis_index("c")
     pad, width = h.shape[1:]
     acc = None
-    for i in range(4):
+    for i, x in enumerate((near0, near1, far0, far1)):
         for k in range(2):
             at = 4 * (2 * (yl if i % 2 == 0 else 1 - yl) + k) + 2 * (c if i < 2 else 1 - c)
             a = jnp.concatenate([h[at], h[at + 1]], axis=1)
-            copies[2 * i + k].wait()
-            term = dot(a, buf[i, k].reshape(-1, 2 * width), 1, 1)
+            term = dot(a, x[4 * k : 4 * k + 4].reshape(-1, 2 * width), 1, 1)
             acc = term if acc is None else acc + term
     acc = acc * scale
     acc = jnp.concatenate([acc[:, b * pad : b * pad + rows] for b in range(acc.shape[1] // pad)], axis=1)
     out[...] = acc.astype(BF)
 
 
-def sigma_call(place, h, near, far, rows, scale):
+def sigma_call(h, near, far, rows, scale):
     pad = h.shape[1]
     width = near[0].shape[3]
     return pl.pallas_call(
         functools.partial(sigma_kernel, scale, rows),
         out_shape=jax.ShapeDtypeStruct((pad, 8 * rows), BF),
-        in_specs=[SMEM, VM] + [ANY] * 4,
+        in_specs=[VM] * 5,
         out_specs=VM,
-        scratch_shapes=[pltpu.VMEM((4, 2, 4, 2, pad, width), BF), pltpu.SemaphoreType.DMA((8,))],
         compiler_params=pltpu.CompilerParams(vmem_limit_bytes=VMEM),
         cost_estimate=pl.CostEstimate(flops=128 * pad * pad * width, bytes_accessed=8 * 2**20, transcendentals=0),
         name="sigma",
-    )(place, h, *near, *far)
+    )(h, *near, *far)
 
 
 def local(green, colloc, core):
     nx = lax.axis_size("orb")
     c, x, tau, yl, z = (lax.axis_index(a) for a in ("c", "orb", "tau", "yl", "z"))
-    place = jnp.stack([x, yl, c, z, yl]).astype(jnp.int32)
     rows, cols = colloc.shape
     pad = 192
     deep = pad + core.shape[0]
@@ -171,7 +172,10 @@
     same, cross = [], []
     for i in range(32):
         for o in range(nx):
-            to = o * 8 + i % 8
+            a = i % 8
+            if (i // 8 - o) % 2:
+                a = 2 * (3 - a // 2) + a % 2
+            to = o * 8 + a
             same.append((i * nx + o, to * nx + i // 8))
             cross.append((i * nx + o, (to ^ 1) * nx + i // 8))
 
@@ -221,9 +225,8 @@
     tall = lax.all_gather(tall, ("orb", "yl", "c"), axis=0, tiled=False)
     tall = tall.reshape(nx, 4, deep, cols)
 
-    inner, zfirst, near0 = inner_call(place, g_own, g_other, ring)
-    turned = jnp.stack([x, 1 - yl, c, z, yl]).astype(jnp.int32)
-    inner, zsecond, near1 = inner_call(turned, g_own, g_other, mate, inner)
+    inner, zfirst, near0 = inner_call(g_own, g_other, ring)
+    inner, zsecond, near1 = inner_call(g_own, g_other, mate, inner)
     zcols = jnp.where(yl == 0, jnp.stack([zfirst, zsecond]), jnp.stack([zsecond, zfirst]))
     zcols = zcols.reshape(nx * cols, quarter)
     near = [near0, near1]
@@ -251,10 +254,8 @@
     kern = (gf * screened[None]).astype(BF)
     kt = jnp.broadcast_to(kern[:, None], (2, 8, quarter, quarter)).reshape(16, quarter, quarter)
     kt = swap(kt, ("tau", "z")).reshape(nx, cols, quarter)
-    half = half_call(tall, kt, pad)
-    half = jnp.broadcast_to(half[None], (nx, 4, pad, quarter))
-    hrow = swap(half.reshape(16, pad, quarter), ("orb", "c", "yl"))
-    return sigma_call(place, hrow, near, far, rows, -1.0 / (nx * cols))[None, :rows]
+    hrow = swap(half_call(tall, kt, pad), ("orb", "c", "yl"))
+    return sigma_call(hrow, near, far, rows, -1.0 / (nx * cols))[None, :rows]
 
 
 def solution(mesh):

time: 233 us -> 226 us (0.970)
  starting transfers between devices: 77.7 us -> 70.6 us
  local copies, waits for them, and re-layouts: 16.6 us -> 13.2 us
    ppermute x11, starting transfers between devices: 23.1 us -> 19 us  [shift(): return lax.ppermute(value, axis, [(i, (i + by) % n) for i in range(n)])]
    all_to_all x4, starting transfers between devices: 32.5 us -> 29.6 us  [swap(): return lax.all_to_all(value, axes, 0, 0, tiled=True)]
    ppermute x11, waiting for transfers between devices: 7.2 us -> 9.73 us  [shift(): return lax.ppermute(value, axis, [(i, (i + by) % n) for i in range(n)])]
  transfers between devices with their start and end apart: 26 -> 26, of which waited for: 12 -> 13; matrix products, arithmetic and copies ran while one was open for 4% -> 3% of each run, Pallas kernels for 6% -> 6%
where the time goes in v3:
time: 226 us; the launch traced here: 225 us
  starting transfers between devices  70.6 us (31%)
  waiting for transfers between devices  65.8 us (29%)
  blocking collectives  34.9 us (15%)
  Pallas kernels  19.1 us (8%)
  between operations  13.9 us (6%)
  local copies, waits for them, and re-layouts  13.2 us (6%)
  matrix products  4.17 us (2%)
  other arithmetic  3.07 us (1%)
    all_to_all x4, waiting for transfers between devices, swap(): return lax.all_to_all(value, axes, 0, 0, tiled=True)  52.8 us
    all_to_all x2, blocking collectives, swap(): return lax.all_to_all(value, axes, 0, 0, tiled=True)  34.9 us
    all_to_all x4, starting transfers between devices, swap(): return lax.all_to_all(value, axes, 0, 0, tiled=True)  29.6 us
    ppermute x11, starting transfers between devices, shift(): return lax.ppermute(value, axis, [(i, (i + by) % n) for i in range(n)])  19 us
    ppermute x8, starting transfers between devices, across(): return lax.ppermute(value, ('yl', 'tau'), way)  18 us
    ppermute x11, waiting for transfers between devices, shift(): return lax.ppermute(value, axis, [(i, (i + by) % n) for i in range(n)])  9.73 us
    pallas_call x2, Pallas kernels, inner_call(): pl.pallas_call(functools.partial(inner_kernel, second), out_shape=(jax.Sh...  8.77 us
    pallas_call x1, Pallas kernels, sigma_call(): pl.pallas_call(functools.partial(sigma_kernel, scale, rows), out_shape=ja...  6.17 us
  transfers between devices with their start and end apart: 26, of which 13 were waited for; matrix products, arithmetic and copies ran while one was open for 3% of the time, Pallas kernels for 6%

profile of v3, /device:TPU:1, one launch (start us, length us, event | category | flops | bytes accessed | tf_op | source)
XLA Modules:
  0.0 224.7 jit_solution(3918908029312328714)
XLA Ops:
  7.7 3.3 %collective-permute-start.1 = (bf16[192,256]{1,0:T(8,128)(2,1)S(1)}, bf16[192,256]{1,0:T(8,128)(2,1)S(1)}, u32[]{:S(2)}, u32[]{:S(2)}) collective-permute-start(bf16[192,256]{1,0:T(8,128)(2,1)S(1)} %get-tuple-element.52), channel_id=1, source_target_pairs={{0,8},{2,120},{4,136},{6,248},{8,0},{10,112},{12,128},{14,240},{16... | collective-permute-start | bytes 294920 | tf_op jit(solution)/shard_map/ppermute | solution.py:188
  12.6 2.3 %reshape_squeeze.3 = bf16[188,8,188]{2,1,0:T(8,128)(2,1)S(1)} reshape(bf16[1,188,1504]{2,1,0:T(8,128)(2,1)} %param.3) | data formatting | bytes 1131008 | tf_op jit(solution)/shard_map/reshape;squeeze | solution.py:196
  15.9 8.0 %collective-permute-start.4 = (bf16[2,256,256]{2,1,0:T(8,128)(2,1)S(1)}, bf16[2,256,256]{2,1,0:T(8,128)(2,1)S(1)}, u32[]{:S(2)}, u32[]{:S(2)}) collective-permute-start(bf16[2,256,256]{2,1,0:T(8,128)(2,1)S(1)} %maximum_select_fusion.1.refs_0_), channel_id=1, source_target_pairs={{0,128},{128,0},{1,129},{129,1},{2,130},{130,2},{3,131},{131,3},{4... | collective-permute-start | bytes 786440 | tf_op jit(solution)/shard_map/ppermute | solution.py:204
  23.9 7.7 %collective-permute-start.5 = (bf16[2,256,256]{2,1,0:T(8,128)(2,1)S(1)}, bf16[2,256,256]{2,1,0:T(8,128)(2,1)S(1)}, u32[]{:S(2)}, u32[]{:S(2)}) collective-permute-start(bf16[2,256,256]{2,1,0:T(8,128)(2,1)S(1)} %maximum_select_fusion.1.refs_0_), channel_id=1, source_target_pairs={{0,112},{16,0},{32,16},{48,32},{64,48},{80,64},{96,80},{112,96},{1... | collective-permute-start | bytes 786440 | tf_op jit(solution)/shard_map/ppermute | solution.py:28
  31.6 2.8 %collective-permute-done.3.refs_1_ = bf16[2,256,256]{2,1,0:T(8,128)(2,1)S(1)} collective-permute-done((bf16[2,256,256]{2,1,0:T(8,128)(2,1)S(1)}, bf16[2,256,256]{2,1,0:T(8,128)(2,1)S(1)}, u32[]{:S(2)}, u32[]{:S(2)}) %collective-permute-start.3) | collective-permute-done | bytes 262176 | tf_op jit(solution)/shard_map/ppermute | solution.py:28
  39.6 3.3 %collective-permute-start.9 = (bf16[2,256,256]{2,1,0:T(8,128)(2,1)S(1)}, bf16[2,256,256]{2,1,0:T(8,128)(2,1)S(1)}, u32[]{:S(2)}, u32[]{:S(2)}) collective-permute-start(bf16[2,256,256]{2,1,0:T(8,128)(2,1)S(1)} %collective-permute-done.5.refs_5_), channel_id=1, source_target_pairs={{0,112},{16,0},{32,16},{48,32},{64,48},{80,64},{96,80},{112,96},{1... | collective-permute-start | bytes 786440 | tf_op jit(solution)/shard_map/ppermute | solution.py:28
  48.2 2.7 %collective-permute-start.14 = (bf16[2,256,256]{2,1,0:T(8,128)(2,1)S(1)}, bf16[2,256,256]{2,1,0:T(8,128)(2,1)S(1)}, u32[]{:S(2)}, u32[]{:S(2)}) collective-permute-start(bf16[2,256,256]{2,1,0:T(8,128)(2,1)S(1)} %collective-permute-done.9.refs_6_), channel_id=1, source_target_pairs={{0,112},{16,0},{32,16},{48,32},{64,48},{80,64},{96,80},{112,96},{1... | collective-permute-start | bytes 786440 | tf_op jit(solution)/shard_map/ppermute | solution.py:28
  50.8 3.7 %collective-permute-start.10 = (bf16[192,1536]{1,0:T(8,128)(2,1)S(1)}, bf16[192,1536]{1,0:T(8,128)(2,1)S(1)}, u32[]{:S(2)}, u32[]{:S(2)}) collective-permute-start(bf16[192,1536]{1,0:T(8,128)(2,1)S(1)} %reshape.56.own), channel_id=1, source_target_pairs={{0,8},{8,0},{1,9},{9,1},{2,10},{10,2},{3,11},{11,3},{4,12},{12,4},... | collective-permute-start | bytes 1769480 | tf_op jit(solution)/shard_map/ppermute | solution.py:28
  58.0 3.0 %collective-permute-done.15.refs_4_ = bf16[2,256,256]{2,1,0:T(8,128)(2,1)S(1)} collective-permute-done((bf16[2,256,256]{2,1,0:T(8,128)(2,1)S(1)}, bf16[2,256,256]{2,1,0:T(8,128)(2,1)S(1)}, u32[]{:S(2)}, u32[]{:S(2)}) %collective-permute-start.15) | collective-permute-done | bytes 262176 | tf_op jit(solution)/shard_map/ppermute | solution.py:28
  65.4 4.2 %inner.2 = (bf16[2,2,2,192,128]{4,3,2,1,0:T(8,128)(2,1)}, bf16[1024,128]{1,0:T(8,128)(2,1)}, bf16[8,2,192,256]{3,2,1,0:T(8,128)(2,1)}) custom-call(bf16[192,1536]{1,0:T(8,128)(2,1)} %copy-done, bf16[192,1536]{1,0:T(8,128)(2,1)} %copy-done.2, bf16[2,256,256]{2,1,0:T(8,128)(2,1)} %copy-done.5, bf16[2,256,256]{2,1,0:T(8,128)(2,1)} %copy-done.15, ...), custom_call_target="tpu_custom_call" | custom-call | flops 603979776 | bytes 6291456 | tf_op jit(solution)/shard_map/inner/pallas_call | solution.py:100
  71.5 4.5 %inner.3 = (bf16[4,2,2,192,128]{4,3,2,1,0:T(8,128)(2,1)}, bf16[1024,128]{1,0:T(8,128)(2,1)}, bf16[8,2,192,256]{3,2,1,0:T(8,128)(2,1)}) custom-call(bf16[192,1536]{1,0:T(8,128)(2,1)} %copy-done, bf16[192,1536]{1,0:T(8,128)(2,1)} %copy-done.2, bf16[2,256,256]{2,1,0:T(8,128)(2,1)} %copy-done.7, bf16[2,256,256]{2,1,0:T(8,128)(2,1)} %copy-done.8, ...), custom_call_target="tpu_custom_call" | custom-call | flops 603979776 | bytes 6291456 | tf_op jit(solution)/shard_map/inner/pallas_call | solution.py:100
  76.0 14.4 %all_to_all.30 = bf16[8,2,192,128]{3,2,1,0:T(8,128)(2,1)S(1)} all-to-all(bf16[8,2,192,128]{3,2,1,0:T(8,128)(2,1)} %bitcast.48), channel_id=1, replica_groups=mesh['yl'=2,'z'=8,'c'=2,'orb'=4,'tau'=2] {'orb','yl'}, dimensions={0} | all-to-all | bytes 1572864 | tf_op jit(solution)/shard_map/all_to_all | solution.py:18
  90.7 3.5 %convolution_convert_fusion = bf16[4,512,128]{2,1,0:T(8,128)(2,1)S(1)} fusion(bf16[4,1024,512]{2,1,0:T(8,128)(2,1)} %bitcast.38, bf16[1024,128,1]{1,0,2:T(8,128)(2,1)S(1)} %bitcast.50), kind=kOutput, calls=%fused_computation | convolution fusion | flops 537133056 | bytes 4980736 | tf_op jit(solution)/shard_map/dot_general | solution.py:241
  94.3 20.4 %all_to_all.31 = bf16[16,128,128]{2,1,0:T(8,128)(2,1)S(1)} all-to-all(bf16[16,128,128]{2,1,0:T(8,128)(2,1)S(1)} %bitcast.49), channel_id=1, replica_groups=mesh['yl'=2,'z'=8,'c'=2,'orb'=4,'tau'=2] {'tau','z'}, dimensions={0} | all-to-all | bytes 1048576 | tf_op jit(solution)/shard_map/all_to_all | solution.py:18
  115.9 12.4 %all-to-all-start.2 = ((bf16[16,128,128]{1,2,0:T(8,128)(2,1)}), bf16[16,128,128]{1,2,0:T(8,128)(2,1)S(1)}, u32[]{:S(2)}, u32[]{:S(2)}) async-start(bf16[16,128,128]{1,2,0:T(8,128)(2,1)} %broadcast_in_dim.11), calls=%async_computation.2 | async-start | bytes 1048576 | tf_op jit(solution)/shard_map/all_to_all | solution.py:18
  128.3 11.0 %all-to-all-done.2 = bf16[16,128,128]{1,2,0:T(8,128)(2,1)S(1)} async-done(((bf16[16,128,128]{1,2,0:T(8,128)(2,1)}), bf16[16,128,128]{1,2,0:T(8,128)(2,1)S(1)}, u32[]{:S(2)}, u32[]{:S(2)}) %all-to-all-start.2) | async-done | bytes 524320 | tf_op jit(solution)/shard_map/all_to_all | solution.py:18
  140.5 4.3 %all-to-all-start.3 = ((bf16[16,128,128]{2,1,0:T(8,128)(2,1)}), bf16[16,128,128]{2,1,0:T(8,128)(2,1)S(1)}, u32[]{:S(2)}, u32[]{:S(2)}) async-start(bf16[16,128,128]{2,1,0:T(8,128)(2,1)} %broadcast_in_dim.12), calls=%async_computation.3 | async-start | bytes 1048576 | tf_op jit(solution)/shard_map/all_to_all | solution.py:18
  146.9 13.1 %all-to-all-done.3 = bf16[16,128,128]{2,1,0:T(8,128)(2,1)S(1)} async-done(((bf16[16,128,128]{2,1,0:T(8,128)(2,1)}), bf16[16,128,128]{2,1,0:T(8,128)(2,1)S(1)}, u32[]{:S(2)}, u32[]{:S(2)}) %all-to-all-start.3) | async-done | bytes 524320 | tf_op jit(solution)/shard_map/all_to_all | solution.py:18
  161.2 6.7 %all-to-all-start.4 = ((bf16[16,128,128]{2,1,0:T(8,128)(2,1)}), bf16[16,128,128]{2,1,0:T(8,128)(2,1)S(1)}, u32[]{:S(2)}, u32[]{:S(2)}) async-start(bf16[16,128,128]{2,1,0:T(8,128)(2,1)} %bitcast.18), calls=%async_computation.4 | async-start | bytes 1048576 | tf_op jit(solution)/shard_map/all_to_all | solution.py:18
  169.0 14.1 %all-to-all-done.4 = bf16[16,128,128]{2,1,0:T(8,128)(2,1)S(1)} async-done(((bf16[16,128,128]{2,1,0:T(8,128)(2,1)}), bf16[16,128,128]{2,1,0:T(8,128)(2,1)S(1)}, u32[]{:S(2)}, u32[]{:S(2)}) %all-to-all-start.4) | async-done | bytes 524320 | tf_op jit(solution)/shard_map/all_to_all | solution.py:18
  183.8 4.1 %half.1 = bf16[16,192,128]{2,1,0:T(8,128)(2,1)} custom-call(bf16[4,4,256,512]{3,2,1,0:T(8,128)(2,1)} %bitcast.40, bf16[4,512,128]{2,1,0:T(8,128)(2,1)} %bitcast.47), custom_call_target="tpu_custom_call" | custom-call | flops 402653184 | bytes 5242880 | tf_op jit(solution)/shard_map/half/pallas_call | solution.py:122
  188.0 6.3 %all-to-all-start.5 = ((bf16[16,192,128]{2,1,0:T(8,128)(2,1)}), bf16[16,192,128]{2,1,0:T(8,128)(2,1)S(1)}, u32[]{:S(2)}, u32[]{:S(2)}) async-start(bf16[16,192,128]{2,1,0:T(8,128)(2,1)} %half.1), calls=%async_computation.5 | async-start | bytes 1572864 | tf_op jit(solution)/shard_map/all_to_all | solution.py:18
  194.2 14.7 %all-to-all-done.5.h = bf16[16,192,128]{2,1,0:T(8,128)(2,1)S(1)} async-done(((bf16[16,192,128]{2,1,0:T(8,128)(2,1)}), bf16[16,192,128]{2,1,0:T(8,128)(2,1)S(1)}, u32[]{:S(2)}, u32[]{:S(2)}) %all-to-all-start.5) | async-done | bytes 786464 | tf_op jit(solution)/shard_map/all_to_all | solution.py:18
  209.8 6.2 %sigma.1 = bf16[192,1504]{1,0:T(8,128)(2,1)} custom-call(bf16[16,192,128]{2,1,0:T(8,128)(2,1)} %copy-done.1, bf16[8,2,192,256]{3,2,1,0:T(8,128)(2,1)} %get-tuple-element.49.near0, bf16[8,2,192,256]{3,2,1,0:T(8,128)(2,1)} %get-tuple-element.50.near1, bf16[8,2,192,256]{3,2,1,0:T(8,128)(2,1)} %collective-permute-done.19.far0, ...), custom_call_target="tpu_custom_call" | custom-call | flops 1207959552 | bytes 8388608 | tf_op jit(solution)/shard_map/sigma/pallas_call | solution.py:151
  (115 shorter events, 34.1 us)
Async XLA Ops:
  6.5 84.2 %all-gather.3.cloned.1.call-start = ((), (), s32[]{:S(2)}) async-start(), calls=%async_computation.6 | async-start | bytes 4456448 | tf_op jit(solution)/shard_map/all_gather | solution.py:225
  7.7 8.1 %collective-permute-start.1 = (bf16[192,256]{1,0:T(8,128)(2,1)S(1)}, bf16[192,256]{1,0:T(8,128)(2,1)S(1)}, u32[]{:S(2)}, u32[]{:S(2)}) collective-permute-start(bf16[192,256]{1,0:T(8,128)(2,1)S(1)} %get-tuple-element.52), channel_id=1, source_target_pairs={{0,8},{2,120},{4,136},{6,248},{8,0},{10,112},{12,128},{14,240},{16... | collective-permute-start | bytes 294920 | tf_op jit(solution)/shard_map/ppermute | solution.py:188
  15.9 18.6 %collective-permute-start.3 = (bf16[2,256,256]{2,1,0:T(8,128)(2,1)S(1)}, bf16[2,256,256]{2,1,0:T(8,128)(2,1)S(1)}, u32[]{:S(2)}, u32[]{:S(2)}) collective-permute-start(bf16[2,256,256]{2,1,0:T(8,128)(2,1)S(1)} %maximum_select_fusion.1.refs_0_), channel_id=1, source_target_pairs={{0,16},{16,32},{32,48},{48,64},{64,80},{80,96},{96,112},{112,0},{1... | collective-permute-start | bytes 786440 | tf_op jit(solution)/shard_map/ppermute | solution.py:28
  15.9 18.5 %collective-permute-start.4 = (bf16[2,256,256]{2,1,0:T(8,128)(2,1)S(1)}, bf16[2,256,256]{2,1,0:T(8,128)(2,1)S(1)}, u32[]{:S(2)}, u32[]{:S(2)}) collective-permute-start(bf16[2,256,256]{2,1,0:T(8,128)(2,1)S(1)} %maximum_select_fusion.1.refs_0_), channel_id=1, source_target_pairs={{0,128},{128,0},{1,129},{129,1},{2,130},{130,2},{3,131},{131,3},{4... | collective-permute-start | bytes 786440 | tf_op jit(solution)/shard_map/ppermute | solution.py:204
  23.9 12.7 %collective-permute-start.5 = (bf16[2,256,256]{2,1,0:T(8,128)(2,1)S(1)}, bf16[2,256,256]{2,1,0:T(8,128)(2,1)S(1)}, u32[]{:S(2)}, u32[]{:S(2)}) collective-permute-start(bf16[2,256,256]{2,1,0:T(8,128)(2,1)S(1)} %maximum_select_fusion.1.refs_0_), channel_id=1, source_target_pairs={{0,112},{16,0},{32,16},{48,32},{64,48},{80,64},{96,80},{112,96},{1... | collective-permute-start | bytes 786440 | tf_op jit(solution)/shard_map/ppermute | solution.py:28
  36.6 8.5 %collective-permute-start.6 = (bf16[2,256,256]{2,1,0:T(8,128)(2,1)S(1)}, bf16[2,256,256]{2,1,0:T(8,128)(2,1)S(1)}, u32[]{:S(2)}, u32[]{:S(2)}) collective-permute-start(bf16[2,256,256]{2,1,0:T(8,128)(2,1)S(1)} %collective-permute-done.3.refs_1_), channel_id=1, source_target_pairs={{0,16},{16,32},{32,48},{48,64},{64,80},{80,96},{96,112},{112,0},{1... | collective-permute-start | bytes 786440 | tf_op jit(solution)/shard_map/ppermute | solution.py:28
  36.6 8.5 %collective-permute-start.7 = (bf16[2,256,256]{2,1,0:T(8,128)(2,1)S(1)}, bf16[2,256,256]{2,1,0:T(8,128)(2,1)S(1)}, u32[]{:S(2)}, u32[]{:S(2)}) collective-permute-start(bf16[2,256,256]{2,1,0:T(8,128)(2,1)S(1)} %collective-permute-done.3.refs_1_), channel_id=1, source_target_pairs={{0,128},{128,0},{1,129},{129,1},{2,130},{130,2},{3,131},{131,3},{4... | collective-permute-start | bytes 786440 | tf_op jit(solution)/shard_map/ppermute | solution.py:204
  38.0 7.8 %collective-permute-start.8 = (bf16[2,256,256]{2,1,0:T(8,128)(2,1)S(1)}, bf16[2,256,256]{2,1,0:T(8,128)(2,1)S(1)}, u32[]{:S(2)}, u32[]{:S(2)}) collective-permute-start(bf16[2,256,256]{2,1,0:T(8,128)(2,1)S(1)} %collective-permute-done.5.refs_5_), channel_id=1, source_target_pairs={{0,129},{129,0},{1,128},{128,1},{2,131},{131,2},{3,130},{130,3},{4... | collective-permute-start | bytes 786440 | tf_op jit(solution)/shard_map/ppermute | solution.py:204
  39.6 6.6 %collective-permute-start.9 = (bf16[2,256,256]{2,1,0:T(8,128)(2,1)S(1)}, bf16[2,256,256]{2,1,0:T(8,128)(2,1)S(1)}, u32[]{:S(2)}, u32[]{:S(2)}) collective-permute-start(bf16[2,256,256]{2,1,0:T(8,128)(2,1)S(1)} %collective-permute-done.5.refs_5_), channel_id=1, source_target_pairs={{0,112},{16,0},{32,16},{48,32},{64,48},{80,64},{96,80},{112,96},{1... | collective-permute-start | bytes 786440 | tf_op jit(solution)/shard_map/ppermute | solution.py:28
  46.2 8.3 %collective-permute-start.11 = (bf16[2,256,256]{2,1,0:T(8,128)(2,1)S(1)}, bf16[2,256,256]{2,1,0:T(8,128)(2,1)S(1)}, u32[]{:S(2)}, u32[]{:S(2)}) collective-permute-start(bf16[2,256,256]{2,1,0:T(8,128)(2,1)S(1)} %collective-permute-done.6.refs_2_), channel_id=1, source_target_pairs={{0,16},{16,32},{32,48},{48,64},{64,80},{80,96},{96,112},{112,0},{1... | collective-permute-start | bytes 786440 | tf_op jit(solution)/shard_map/ppermute | solution.py:28
  46.3 8.2 %collective-permute-start.12 = (bf16[2,256,256]{2,1,0:T(8,128)(2,1)S(1)}, bf16[2,256,256]{2,1,0:T(8,128)(2,1)S(1)}, u32[]{:S(2)}, u32[]{:S(2)}) collective-permute-start(bf16[2,256,256]{2,1,0:T(8,128)(2,1)S(1)} %collective-permute-done.6.refs_2_), channel_id=1, source_target_pairs={{0,128},{128,0},{1,129},{129,1},{2,130},{130,2},{3,131},{131,3},{4... | collective-permute-start | bytes 786440 | tf_op jit(solution)/shard_map/ppermute | solution.py:204
  46.9 7.6 %collective-permute-start.13 = (bf16[2,256,256]{2,1,0:T(8,128)(2,1)S(1)}, bf16[2,256,256]{2,1,0:T(8,128)(2,1)S(1)}, u32[]{:S(2)}, u32[]{:S(2)}) collective-permute-start(bf16[2,256,256]{2,1,0:T(8,128)(2,1)S(1)} %collective-permute-done.9.refs_6_), channel_id=1, source_target_pairs={{0,129},{129,0},{1,128},{128,1},{2,131},{131,2},{3,130},{130,3},{4... | collective-permute-start | bytes 786440 | tf_op jit(solution)/shard_map/ppermute | solution.py:204
  48.2 6.4 %collective-permute-start.14 = (bf16[2,256,256]{2,1,0:T(8,128)(2,1)S(1)}, bf16[2,256,256]{2,1,0:T(8,128)(2,1)S(1)}, u32[]{:S(2)}, u32[]{:S(2)}) collective-permute-start(bf16[2,256,256]{2,1,0:T(8,128)(2,1)S(1)} %collective-permute-done.9.refs_6_), channel_id=1, source_target_pairs={{0,112},{16,0},{32,16},{48,32},{64,48},{80,64},{96,80},{112,96},{1... | collective-permute-start | bytes 786440 | tf_op jit(solution)/shard_map/ppermute | solution.py:28
  50.8 13.6 %collective-permute-start.10 = (bf16[192,1536]{1,0:T(8,128)(2,1)S(1)}, bf16[192,1536]{1,0:T(8,128)(2,1)S(1)}, u32[]{:S(2)}, u32[]{:S(2)}) collective-permute-start(bf16[192,1536]{1,0:T(8,128)(2,1)S(1)} %reshape.56.own), channel_id=1, source_target_pairs={{0,8},{8,0},{1,9},{9,1},{2,10},{10,2},{3,11},{11,3},{4,12},{12,4},... | collective-permute-start | bytes 1769480 | tf_op jit(solution)/shard_map/ppermute | solution.py:28
  54.6 6.5 %collective-permute-start.15 = (bf16[2,256,256]{2,1,0:T(8,128)(2,1)S(1)}, bf16[2,256,256]{2,1,0:T(8,128)(2,1)S(1)}, u32[]{:S(2)}, u32[]{:S(2)}) collective-permute-start(bf16[2,256,256]{2,1,0:T(8,128)(2,1)S(1)} %collective-permute-done.11.refs_3_), channel_id=1, source_target_pairs={{0,16},{16,32},{32,48},{48,64},{64,80},{80,96},{96,112},{112,0},{1... | collective-permute-start | bytes 786440 | tf_op jit(solution)/shard_map/ppermute | solution.py:28
  54.9 6.4 %collective-permute-start.16 = (bf16[2,256,256]{2,1,0:T(8,128)(2,1)S(1)}, bf16[2,256,256]{2,1,0:T(8,128)(2,1)S(1)}, u32[]{:S(2)}, u32[]{:S(2)}) collective-permute-start(bf16[2,256,256]{2,1,0:T(8,128)(2,1)S(1)} %collective-permute-done.11.refs_3_), channel_id=1, source_target_pairs={{0,128},{128,0},{1,129},{129,1},{2,130},{130,2},{3,131},{131,3},{4... | collective-permute-start | bytes 786440 | tf_op jit(solution)/shard_map/ppermute | solution.py:204
  56.0 6.4 %collective-permute-start.17 = (bf16[2,256,256]{2,1,0:T(8,128)(2,1)S(1)}, bf16[2,256,256]{2,1,0:T(8,128)(2,1)S(1)}, u32[]{:S(2)}, u32[]{:S(2)}) collective-permute-start(bf16[2,256,256]{2,1,0:T(8,128)(2,1)S(1)} %collective-permute-done.14.refs_7_), channel_id=1, source_target_pairs={{0,129},{129,0},{1,128},{128,1},{2,131},{131,2},{3,130},{130,3},{4... | collective-permute-start | bytes 786440 | tf_op jit(solution)/shard_map/ppermute | solution.py:204
  62.5 8.3 %collective-permute-start.18 = (bf16[2,256,256]{2,1,0:T(8,128)(2,1)S(1)}, bf16[2,256,256]{2,1,0:T(8,128)(2,1)S(1)}, u32[]{:S(2)}, u32[]{:S(2)}) collective-permute-start(bf16[2,256,256]{2,1,0:T(8,128)(2,1)S(1)} %collective-permute-done.15.refs_4_), channel_id=1, source_target_pairs={{0,129},{129,0},{1,128},{128,1},{2,131},{131,2},{3,130},{130,3},{4... | collective-permute-start | bytes 786440 | tf_op jit(solution)/shard_map/ppermute | solution.py:204
  115.9 23.4 %all-to-all-start.2 = ((bf16[16,128,128]{1,2,0:T(8,128)(2,1)}), bf16[16,128,128]{1,2,0:T(8,128)(2,1)S(1)}, u32[]{:S(2)}, u32[]{:S(2)}) async-start(bf16[16,128,128]{1,2,0:T(8,128)(2,1)} %broadcast_in_dim.11), calls=%async_computation.2 | async-start | bytes 1048576 | tf_op jit(solution)/shard_map/all_to_all | solution.py:18
  140.5 19.5 %all-to-all-start.3 = ((bf16[16,128,128]{2,1,0:T(8,128)(2,1)}), bf16[16,128,128]{2,1,0:T(8,128)(2,1)S(1)}, u32[]{:S(2)}, u32[]{:S(2)}) async-start(bf16[16,128,128]{2,1,0:T(8,128)(2,1)} %broadcast_in_dim.12), calls=%async_computation.3 | async-start | bytes 1048576 | tf_op jit(solution)/shard_map/all_to_all | solution.py:18
  161.2 21.9 %all-to-all-start.4 = ((bf16[16,128,128]{2,1,0:T(8,128)(2,1)}), bf16[16,128,128]{2,1,0:T(8,128)(2,1)S(1)}, u32[]{:S(2)}, u32[]{:S(2)}) async-start(bf16[16,128,128]{2,1,0:T(8,128)(2,1)} %bitcast.18), calls=%async_computation.4 | async-start | bytes 1048576 | tf_op jit(solution)/shard_map/all_to_all | solution.py:18
  167.9 26.3 %collective-permute-start.19 = (bf16[8,2,192,256]{3,2,1,0:T(8,128)(2,1)S(1)}, bf16[8,2,192,256]{3,2,1,0:T(8,128)(2,1)}, u32[]{:S(2)}, u32[]{:S(2)}) collective-permute-start(bf16[8,2,192,256]{3,2,1,0:T(8,128)(2,1)S(1)} %copy-done.4), channel_id=1, source_target_pairs={{0,8},{8,0},{1,9},{9,1},{2,10},{10,2},{3,11},{11,3},{4,12},{12,4},... | collective-permute-start | bytes 4718600 | tf_op jit(solution)/shard_map/ppermute | solution.py:28
  168.9 25.4 %collective-permute-start.20 = (bf16[8,2,192,256]{3,2,1,0:T(8,128)(2,1)}, bf16[8,2,192,256]{3,2,1,0:T(8,128)(2,1)}, u32[]{:S(2)}, u32[]{:S(2)}) collective-permute-start(bf16[8,2,192,256]{3,2,1,0:T(8,128)(2,1)} %get-tuple-element.50.near1), channel_id=1, source_target_pairs={{0,8},{8,0},{1,9},{9,1},{2,10},{10,2},{3,11},{11,3},{4,12},{12,4},... | collective-permute-start | bytes 4718600 | tf_op jit(solution)/shard_map/ppermute | solution.py:28
  188.0 20.9 %all-to-all-start.5 = ((bf16[16,192,128]{2,1,0:T(8,128)(2,1)}), bf16[16,192,128]{2,1,0:T(8,128)(2,1)S(1)}, u32[]{:S(2)}, u32[]{:S(2)}) async-start(bf16[16,192,128]{2,1,0:T(8,128)(2,1)} %half.1), calls=%async_computation.5 | async-start | bytes 1572864 | tf_op jit(solution)/shard_map/all_to_all | solution.py:18
  (27 other events, 536.1 us)
Sparse Core Ops, SparseCore 0:
  46.3 43.6 all-gather.2

commit v4 on v3

--- a/solution.py
+++ b/solution.py
@@ -138,11 +138,11 @@
         for k in range(2):
             at = 4 * (2 * (yl if i % 2 == 0 else 1 - yl) + k) + 2 * (c if i < 2 else 1 - c)
             a = jnp.concatenate([h[at], h[at + 1]], axis=1)
-            term = dot(a, x[4 * k : 4 * k + 4].reshape(-1, 2 * width), 1, 1)
+            term = dot(x[4 * k : 4 * k + 4].reshape(-1, 2 * width), a, 1, 1)
             acc = term if acc is None else acc + term
-    acc = acc * scale
+    acc = (acc * scale).T
     acc = jnp.concatenate([acc[:, b * pad : b * pad + rows] for b in range(acc.shape[1] // pad)], axis=1)
-    out[...] = acc.astype(BF)
+    out[...] = acc[:rows].astype(BF)
 
 
 def sigma_call(h, near, far, rows, scale):
@@ -150,7 +150,7 @@
     width = near[0].shape[3]
     return pl.pallas_call(
         functools.partial(sigma_kernel, scale, rows),
-        out_shape=jax.ShapeDtypeStruct((pad, 8 * rows), BF),
+        out_shape=jax.ShapeDtypeStruct((rows, 8 * rows), BF),
         in_specs=[VM] * 5,
         out_specs=VM,
         compiler_params=pltpu.CompilerParams(vmem_limit_bytes=VMEM),
@@ -255,7 +255,7 @@
     kt = jnp.broadcast_to(kern[:, None], (2, 8, quarter, quarter)).reshape(16, quarter, quarter)
     kt = swap(kt, ("tau", "z")).reshape(nx, cols, quarter)
     hrow = swap(half_call(tall, kt, pad), ("orb", "c", "yl"))
-    return sigma_call(hrow, near, far, rows, -1.0 / (nx * cols))[None, :rows]
+    return sigma_call(hrow, near, far, rows, -1.0 / (nx * cols))[None]
 
 
 def solution(mesh):

time: 226 us -> 224 us (level)
  no operation moved by 1% of the time
where the time goes in v4:
time: 224 us; the launch traced here: 223 us
  starting transfers between devices  70.6 us (32%)
  waiting for transfers between devices  65.8 us (29%)
  blocking collectives  34.9 us (16%)
  Pallas kernels  19 us (8%)
  between operations  13.9 us (6%)
  local copies, waits for them, and re-layouts  11.3 us (5%)
  matrix products  4.17 us (2%)
  other arithmetic  3.07 us (1%)
    all_to_all x4, waiting for transfers between devices, swap(): return lax.all_to_all(value, axes, 0, 0, tiled=True)  52.8 us
    all_to_all x2, blocking collectives, swap(): return lax.all_to_all(value, axes, 0, 0, tiled=True)  34.9 us
    all_to_all x4, starting transfers between devices, swap(): return lax.all_to_all(value, axes, 0, 0, tiled=True)  29.6 us
    ppermute x11, starting transfers between devices, shift(): return lax.ppermute(value, axis, [(i, (i + by) % n) for i in range(n)])  19 us
    ppermute x8, starting transfers between devices, across(): return lax.ppermute(value, ('yl', 'tau'), way)  18 us
    ppermute x11, waiting for transfers between devices, shift(): return lax.ppermute(value, axis, [(i, (i + by) % n) for i in range(n)])  9.73 us
    pallas_call x2, Pallas kernels, inner_call(): pl.pallas_call(functools.partial(inner_kernel, second), out_shape=(jax.Sh...  8.77 us
    pallas_call x1, Pallas kernels, sigma_call(): pl.pallas_call(functools.partial(sigma_kernel, scale, rows), out_shape=ja...  6.1 us
  transfers between devices with their start and end apart: 26, of which 13 were waited for; matrix products, arithmetic and copies ran while one was open for 3% of the time, Pallas kernels for 6%

profile of v4, /device:TPU:1, one launch (start us, length us, event | category | flops | bytes accessed | tf_op | source)
XLA Modules:
  0.0 222.7 jit_solution(18007552606466892570)
XLA Ops:
  7.7 3.3 %collective-permute-start.1 = (bf16[192,256]{1,0:T(8,128)(2,1)S(1)}, bf16[192,256]{1,0:T(8,128)(2,1)S(1)}, u32[]{:S(2)}, u32[]{:S(2)}) collective-permute-start(bf16[192,256]{1,0:T(8,128)(2,1)S(1)} %get-tuple-element.52), channel_id=1, source_target_pairs={{0,8},{2,120},{4,136},{6,248},{8,0},{10,112},{12,128},{14,240},{16... | collective-permute-start | bytes 294920 | tf_op jit(solution)/shard_map/ppermute | solution.py:188
  12.6 2.3 %reshape_squeeze.3 = bf16[188,8,188]{2,1,0:T(8,128)(2,1)S(1)} reshape(bf16[1,188,1504]{2,1,0:T(8,128)(2,1)} %param.3) | data formatting | bytes 1131008 | tf_op jit(solution)/shard_map/reshape;squeeze | solution.py:196
  15.9 8.0 %collective-permute-start.4 = (bf16[2,256,256]{2,1,0:T(8,128)(2,1)S(1)}, bf16[2,256,256]{2,1,0:T(8,128)(2,1)S(1)}, u32[]{:S(2)}, u32[]{:S(2)}) collective-permute-start(bf16[2,256,256]{2,1,0:T(8,128)(2,1)S(1)} %maximum_select_fusion.1.refs_0_), channel_id=1, source_target_pairs={{0,128},{128,0},{1,129},{129,1},{2,130},{130,2},{3,131},{131,3},{4... | collective-permute-start | bytes 786440 | tf_op jit(solution)/shard_map/ppermute | solution.py:204
  23.9 7.7 %collective-permute-start.5 = (bf16[2,256,256]{2,1,0:T(8,128)(2,1)S(1)}, bf16[2,256,256]{2,1,0:T(8,128)(2,1)S(1)}, u32[]{:S(2)}, u32[]{:S(2)}) collective-permute-start(bf16[2,256,256]{2,1,0:T(8,128)(2,1)S(1)} %maximum_select_fusion.1.refs_0_), channel_id=1, source_target_pairs={{0,112},{16,0},{32,16},{48,32},{64,48},{80,64},{96,80},{112,96},{1... | collective-permute-start | bytes 786440 | tf_op jit(solution)/shard_map/ppermute | solution.py:28
  31.6 2.8 %collective-permute-done.3.refs_1_ = bf16[2,256,256]{2,1,0:T(8,128)(2,1)S(1)} collective-permute-done((bf16[2,256,256]{2,1,0:T(8,128)(2,1)S(1)}, bf16[2,256,256]{2,1,0:T(8,128)(2,1)S(1)}, u32[]{:S(2)}, u32[]{:S(2)}) %collective-permute-start.3) | collective-permute-done | bytes 262176 | tf_op jit(solution)/shard_map/ppermute | solution.py:28
  39.6 3.3 %collective-permute-start.9 = (bf16[2,256,256]{2,1,0:T(8,128)(2,1)S(1)}, bf16[2,256,256]{2,1,0:T(8,128)(2,1)S(1)}, u32[]{:S(2)}, u32[]{:S(2)}) collective-permute-start(bf16[2,256,256]{2,1,0:T(8,128)(2,1)S(1)} %collective-permute-done.5.refs_5_), channel_id=1, source_target_pairs={{0,112},{16,0},{32,16},{48,32},{64,48},{80,64},{96,80},{112,96},{1... | collective-permute-start | bytes 786440 | tf_op jit(solution)/shard_map/ppermute | solution.py:28
  48.2 2.7 %collective-permute-start.14 = (bf16[2,256,256]{2,1,0:T(8,128)(2,1)S(1)}, bf16[2,256,256]{2,1,0:T(8,128)(2,1)S(1)}, u32[]{:S(2)}, u32[]{:S(2)}) collective-permute-start(bf16[2,256,256]{2,1,0:T(8,128)(2,1)S(1)} %collective-permute-done.9.refs_6_), channel_id=1, source_target_pairs={{0,112},{16,0},{32,16},{48,32},{64,48},{80,64},{96,80},{112,96},{1... | collective-permute-start | bytes 786440 | tf_op jit(solution)/shard_map/ppermute | solution.py:28
  50.8 3.7 %collective-permute-start.10 = (bf16[192,1536]{1,0:T(8,128)(2,1)S(1)}, bf16[192,1536]{1,0:T(8,128)(2,1)S(1)}, u32[]{:S(2)}, u32[]{:S(2)}) collective-permute-start(bf16[192,1536]{1,0:T(8,128)(2,1)S(1)} %reshape.56.own), channel_id=1, source_target_pairs={{0,8},{8,0},{1,9},{9,1},{2,10},{10,2},{3,11},{11,3},{4,12},{12,4},... | collective-permute-start | bytes 1769480 | tf_op jit(solution)/shard_map/ppermute | solution.py:28
  58.0 3.0 %collective-permute-done.15.refs_4_ = bf16[2,256,256]{2,1,0:T(8,128)(2,1)S(1)} collective-permute-done((bf16[2,256,256]{2,1,0:T(8,128)(2,1)S(1)}, bf16[2,256,256]{2,1,0:T(8,128)(2,1)S(1)}, u32[]{:S(2)}, u32[]{:S(2)}) %collective-permute-start.15) | collective-permute-done | bytes 262176 | tf_op jit(solution)/shard_map/ppermute | solution.py:28
  65.4 4.2 %inner.2 = (bf16[2,2,2,192,128]{4,3,2,1,0:T(8,128)(2,1)}, bf16[1024,128]{1,0:T(8,128)(2,1)}, bf16[8,2,192,256]{3,2,1,0:T(8,128)(2,1)}) custom-call(bf16[192,1536]{1,0:T(8,128)(2,1)} %copy-done, bf16[192,1536]{1,0:T(8,128)(2,1)} %copy-done.2, bf16[2,256,256]{2,1,0:T(8,128)(2,1)} %copy-done.5, bf16[2,256,256]{2,1,0:T(8,128)(2,1)} %copy-done.15, ...), custom_call_target="tpu_custom_call" | custom-call | flops 603979776 | bytes 6291456 | tf_op jit(solution)/shard_map/inner/pallas_call | solution.py:100
  71.5 4.5 %inner.3 = (bf16[4,2,2,192,128]{4,3,2,1,0:T(8,128)(2,1)}, bf16[1024,128]{1,0:T(8,128)(2,1)}, bf16[8,2,192,256]{3,2,1,0:T(8,128)(2,1)}) custom-call(bf16[192,1536]{1,0:T(8,128)(2,1)} %copy-done, bf16[192,1536]{1,0:T(8,128)(2,1)} %copy-done.2, bf16[2,256,256]{2,1,0:T(8,128)(2,1)} %copy-done.7, bf16[2,256,256]{2,1,0:T(8,128)(2,1)} %copy-done.8, ...), custom_call_target="tpu_custom_call" | custom-call | flops 603979776 | bytes 6291456 | tf_op jit(solution)/shard_map/inner/pallas_call | solution.py:100
  76.0 14.4 %all_to_all.30 = bf16[8,2,192,128]{3,2,1,0:T(8,128)(2,1)S(1)} all-to-all(bf16[8,2,192,128]{3,2,1,0:T(8,128)(2,1)} %bitcast.47), channel_id=1, replica_groups=mesh['yl'=2,'z'=8,'c'=2,'orb'=4,'tau'=2] {'orb','yl'}, dimensions={0} | all-to-all | bytes 1572864 | tf_op jit(solution)/shard_map/all_to_all | solution.py:18
  90.7 3.5 %convolution_convert_fusion = bf16[4,512,128]{2,1,0:T(8,128)(2,1)S(1)} fusion(bf16[4,1024,512]{2,1,0:T(8,128)(2,1)} %bitcast.37, bf16[1024,128,1]{1,0,2:T(8,128)(2,1)S(1)} %bitcast.49), kind=kOutput, calls=%fused_computation | convolution fusion | flops 537133056 | bytes 4980736 | tf_op jit(solution)/shard_map/dot_general | solution.py:241
  94.3 20.4 %all_to_all.31 = bf16[16,128,128]{2,1,0:T(8,128)(2,1)S(1)} all-to-all(bf16[16,128,128]{2,1,0:T(8,128)(2,1)S(1)} %bitcast.48), channel_id=1, replica_groups=mesh['yl'=2,'z'=8,'c'=2,'orb'=4,'tau'=2] {'tau','z'}, dimensions={0} | all-to-all | bytes 1048576 | tf_op jit(solution)/shard_map/all_to_all | solution.py:18
  115.9 12.4 %all-to-all-start.2 = ((bf16[16,128,128]{1,2,0:T(8,128)(2,1)}), bf16[16,128,128]{1,2,0:T(8,128)(2,1)S(1)}, u32[]{:S(2)}, u32[]{:S(2)}) async-start(bf16[16,128,128]{1,2,0:T(8,128)(2,1)} %broadcast_in_dim.11), calls=%async_computation.2 | async-start | bytes 1048576 | tf_op jit(solution)/shard_map/all_to_all | solution.py:18
  128.3 11.0 %all-to-all-done.2 = bf16[16,128,128]{1,2,0:T(8,128)(2,1)S(1)} async-done(((bf16[16,128,128]{1,2,0:T(8,128)(2,1)}), bf16[16,128,128]{1,2,0:T(8,128)(2,1)S(1)}, u32[]{:S(2)}, u32[]{:S(2)}) %all-to-all-start.2) | async-done | bytes 524320 | tf_op jit(solution)/shard_map/all_to_all | solution.py:18
  140.5 4.3 %all-to-all-start.3 = ((bf16[16,128,128]{2,1,0:T(8,128)(2,1)}), bf16[16,128,128]{2,1,0:T(8,128)(2,1)S(1)}, u32[]{:S(2)}, u32[]{:S(2)}) async-start(bf16[16,128,128]{2,1,0:T(8,128)(2,1)} %broadcast_in_dim.12), calls=%async_computation.3 | async-start | bytes 1048576 | tf_op jit(solution)/shard_map/all_to_all | solution.py:18
  146.9 13.1 %all-to-all-done.3 = bf16[16,128,128]{2,1,0:T(8,128)(2,1)S(1)} async-done(((bf16[16,128,128]{2,1,0:T(8,128)(2,1)}), bf16[16,128,128]{2,1,0:T(8,128)(2,1)S(1)}, u32[]{:S(2)}, u32[]{:S(2)}) %all-to-all-start.3) | async-done | bytes 524320 | tf_op jit(solution)/shard_map/all_to_all | solution.py:18
  161.2 6.7 %all-to-all-start.4 = ((bf16[16,128,128]{2,1,0:T(8,128)(2,1)}), bf16[16,128,128]{2,1,0:T(8,128)(2,1)S(1)}, u32[]{:S(2)}, u32[]{:S(2)}) async-start(bf16[16,128,128]{2,1,0:T(8,128)(2,1)} %bitcast.18), calls=%async_computation.4 | async-start | bytes 1048576 | tf_op jit(solution)/shard_map/all_to_all | solution.py:18
  169.0 14.1 %all-to-all-done.4 = bf16[16,128,128]{2,1,0:T(8,128)(2,1)S(1)} async-done(((bf16[16,128,128]{2,1,0:T(8,128)(2,1)}), bf16[16,128,128]{2,1,0:T(8,128)(2,1)S(1)}, u32[]{:S(2)}, u32[]{:S(2)}) %all-to-all-start.4) | async-done | bytes 524320 | tf_op jit(solution)/shard_map/all_to_all | solution.py:18
  183.8 4.1 %half.1 = bf16[16,192,128]{2,1,0:T(8,128)(2,1)} custom-call(bf16[4,4,256,512]{3,2,1,0:T(8,128)(2,1)} %bitcast.39, bf16[4,512,128]{2,1,0:T(8,128)(2,1)} %bitcast.46), custom_call_target="tpu_custom_call" | custom-call | flops 402653184 | bytes 5242880 | tf_op jit(solution)/shard_map/half/pallas_call | solution.py:122
  188.0 6.3 %all-to-all-start.5 = ((bf16[16,192,128]{2,1,0:T(8,128)(2,1)}), bf16[16,192,128]{2,1,0:T(8,128)(2,1)S(1)}, u32[]{:S(2)}, u32[]{:S(2)}) async-start(bf16[16,192,128]{2,1,0:T(8,128)(2,1)} %half.1), calls=%async_computation.5 | async-start | bytes 1572864 | tf_op jit(solution)/shard_map/all_to_all | solution.py:18
  194.2 14.7 %all-to-all-done.5.h = bf16[16,192,128]{2,1,0:T(8,128)(2,1)S(1)} async-done(((bf16[16,192,128]{2,1,0:T(8,128)(2,1)}), bf16[16,192,128]{2,1,0:T(8,128)(2,1)S(1)}, u32[]{:S(2)}, u32[]{:S(2)}) %all-to-all-start.5) | async-done | bytes 786464 | tf_op jit(solution)/shard_map/all_to_all | solution.py:18
  209.8 6.1 %sigma.1 = bf16[188,1504]{1,0:T(8,128)(2,1)} custom-call(bf16[16,192,128]{2,1,0:T(8,128)(2,1)} %copy-done.1, bf16[8,2,192,256]{3,2,1,0:T(8,128)(2,1)} %get-tuple-element.49.near0, bf16[8,2,192,256]{3,2,1,0:T(8,128)(2,1)} %get-tuple-element.50.near1, bf16[8,2,192,256]{3,2,1,0:T(8,128)(2,1)} %collective-permute-done.19.far0, ...), custom_call_target="tpu_custom_call" | custom-call | flops 1207959552 | bytes 8388608 | tf_op jit(solution)/shard_map/sigma/pallas_call | solution.py:151
  (114 shorter events, 32.2 us)
Async XLA Ops:
  6.5 84.2 %all-gather.3.cloned.1.call-start = ((), (), s32[]{:S(2)}) async-start(), calls=%async_computation.6 | async-start | bytes 4456448 | tf_op jit(solution)/shard_map/all_gather | solution.py:225
  7.7 8.1 %collective-permute-start.1 = (bf16[192,256]{1,0:T(8,128)(2,1)S(1)}, bf16[192,256]{1,0:T(8,128)(2,1)S(1)}, u32[]{:S(2)}, u32[]{:S(2)}) collective-permute-start(bf16[192,256]{1,0:T(8,128)(2,1)S(1)} %get-tuple-element.52), channel_id=1, source_target_pairs={{0,8},{2,120},{4,136},{6,248},{8,0},{10,112},{12,128},{14,240},{16... | collective-permute-start | bytes 294920 | tf_op jit(solution)/shard_map/ppermute | solution.py:188
  15.9 18.6 %collective-permute-start.3 = (bf16[2,256,256]{2,1,0:T(8,128)(2,1)S(1)}, bf16[2,256,256]{2,1,0:T(8,128)(2,1)S(1)}, u32[]{:S(2)}, u32[]{:S(2)}) collective-permute-start(bf16[2,256,256]{2,1,0:T(8,128)(2,1)S(1)} %maximum_select_fusion.1.refs_0_), channel_id=1, source_target_pairs={{0,16},{16,32},{32,48},{48,64},{64,80},{80,96},{96,112},{112,0},{1... | collective-permute-start | bytes 786440 | tf_op jit(solution)/shard_map/ppermute | solution.py:28
  15.9 18.5 %collective-permute-start.4 = (bf16[2,256,256]{2,1,0:T(8,128)(2,1)S(1)}, bf16[2,256,256]{2,1,0:T(8,128)(2,1)S(1)}, u32[]{:S(2)}, u32[]{:S(2)}) collective-permute-start(bf16[2,256,256]{2,1,0:T(8,128)(2,1)S(1)} %maximum_select_fusion.1.refs_0_), channel_id=1, source_target_pairs={{0,128},{128,0},{1,129},{129,1},{2,130},{130,2},{3,131},{131,3},{4... | collective-permute-start | bytes 786440 | tf_op jit(solution)/shard_map/ppermute | solution.py:204
  23.9 12.7 %collective-permute-start.5 = (bf16[2,256,256]{2,1,0:T(8,128)(2,1)S(1)}, bf16[2,256,256]{2,1,0:T(8,128)(2,1)S(1)}, u32[]{:S(2)}, u32[]{:S(2)}) collective-permute-start(bf16[2,256,256]{2,1,0:T(8,128)(2,1)S(1)} %maximum_select_fusion.1.refs_0_), channel_id=1, source_target_pairs={{0,112},{16,0},{32,16},{48,32},{64,48},{80,64},{96,80},{112,96},{1... | collective-permute-start | bytes 786440 | tf_op jit(solution)/shard_map/ppermute | solution.py:28
  36.6 8.5 %collective-permute-start.6 = (bf16[2,256,256]{2,1,0:T(8,128)(2,1)S(1)}, bf16[2,256,256]{2,1,0:T(8,128)(2,1)S(1)}, u32[]{:S(2)}, u32[]{:S(2)}) collective-permute-start(bf16[2,256,256]{2,1,0:T(8,128)(2,1)S(1)} %collective-permute-done.3.refs_1_), channel_id=1, source_target_pairs={{0,16},{16,32},{32,48},{48,64},{64,80},{80,96},{96,112},{112,0},{1... | collective-permute-start | bytes 786440 | tf_op jit(solution)/shard_map/ppermute | solution.py:28
  36.6 8.5 %collective-permute-start.7 = (bf16[2,256,256]{2,1,0:T(8,128)(2,1)S(1)}, bf16[2,256,256]{2,1,0:T(8,128)(2,1)S(1)}, u32[]{:S(2)}, u32[]{:S(2)}) collective-permute-start(bf16[2,256,256]{2,1,0:T(8,128)(2,1)S(1)} %collective-permute-done.3.refs_1_), channel_id=1, source_target_pairs={{0,128},{128,0},{1,129},{129,1},{2,130},{130,2},{3,131},{131,3},{4... | collective-permute-start | bytes 786440 | tf_op jit(solution)/shard_map/ppermute | solution.py:204
  38.0 7.8 %collective-permute-start.8 = (bf16[2,256,256]{2,1,0:T(8,128)(2,1)S(1)}, bf16[2,256,256]{2,1,0:T(8,128)(2,1)S(1)}, u32[]{:S(2)}, u32[]{:S(2)}) collective-permute-start(bf16[2,256,256]{2,1,0:T(8,128)(2,1)S(1)} %collective-permute-done.5.refs_5_), channel_id=1, source_target_pairs={{0,129},{129,0},{1,128},{128,1},{2,131},{131,2},{3,130},{130,3},{4... | collective-permute-start | bytes 786440 | tf_op jit(solution)/shard_map/ppermute | solution.py:204
  39.6 6.6 %collective-permute-start.9 = (bf16[2,256,256]{2,1,0:T(8,128)(2,1)S(1)}, bf16[2,256,256]{2,1,0:T(8,128)(2,1)S(1)}, u32[]{:S(2)}, u32[]{:S(2)}) collective-permute-start(bf16[2,256,256]{2,1,0:T(8,128)(2,1)S(1)} %collective-permute-done.5.refs_5_), channel_id=1, source_target_pairs={{0,112},{16,0},{32,16},{48,32},{64,48},{80,64},{96,80},{112,96},{1... | collective-permute-start | bytes 786440 | tf_op jit(solution)/shard_map/ppermute | solution.py:28
  46.2 8.3 %collective-permute-start.11 = (bf16[2,256,256]{2,1,0:T(8,128)(2,1)S(1)}, bf16[2,256,256]{2,1,0:T(8,128)(2,1)S(1)}, u32[]{:S(2)}, u32[]{:S(2)}) collective-permute-start(bf16[2,256,256]{2,1,0:T(8,128)(2,1)S(1)} %collective-permute-done.6.refs_2_), channel_id=1, source_target_pairs={{0,16},{16,32},{32,48},{48,64},{64,80},{80,96},{96,112},{112,0},{1... | collective-permute-start | bytes 786440 | tf_op jit(solution)/shard_map/ppermute | solution.py:28
  46.3 8.2 %collective-permute-start.12 = (bf16[2,256,256]{2,1,0:T(8,128)(2,1)S(1)}, bf16[2,256,256]{2,1,0:T(8,128)(2,1)S(1)}, u32[]{:S(2)}, u32[]{:S(2)}) collective-permute-start(bf16[2,256,256]{2,1,0:T(8,128)(2,1)S(1)} %collective-permute-done.6.refs_2_), channel_id=1, source_target_pairs={{0,128},{128,0},{1,129},{129,1},{2,130},{130,2},{3,131},{131,3},{4... | collective-permute-start | bytes 786440 | tf_op jit(solution)/shard_map/ppermute | solution.py:204
  46.9 7.6 %collective-permute-start.13 = (bf16[2,256,256]{2,1,0:T(8,128)(2,1)S(1)}, bf16[2,256,256]{2,1,0:T(8,128)(2,1)S(1)}, u32[]{:S(2)}, u32[]{:S(2)}) collective-permute-start(bf16[2,256,256]{2,1,0:T(8,128)(2,1)S(1)} %collective-permute-done.9.refs_6_), channel_id=1, source_target_pairs={{0,129},{129,0},{1,128},{128,1},{2,131},{131,2},{3,130},{130,3},{4... | collective-permute-start | bytes 786440 | tf_op jit(solution)/shard_map/ppermute | solution.py:204
  48.2 6.4 %collective-permute-start.14 = (bf16[2,256,256]{2,1,0:T(8,128)(2,1)S(1)}, bf16[2,256,256]{2,1,0:T(8,128)(2,1)S(1)}, u32[]{:S(2)}, u32[]{:S(2)}) collective-permute-start(bf16[2,256,256]{2,1,0:T(8,128)(2,1)S(1)} %collective-permute-done.9.refs_6_), channel_id=1, source_target_pairs={{0,112},{16,0},{32,16},{48,32},{64,48},{80,64},{96,80},{112,96},{1... | collective-permute-start | bytes 786440 | tf_op jit(solution)/shard_map/ppermute | solution.py:28
  50.8 13.6 %collective-permute-start.10 = (bf16[192,1536]{1,0:T(8,128)(2,1)S(1)}, bf16[192,1536]{1,0:T(8,128)(2,1)S(1)}, u32[]{:S(2)}, u32[]{:S(2)}) collective-permute-start(bf16[192,1536]{1,0:T(8,128)(2,1)S(1)} %reshape.56.own), channel_id=1, source_target_pairs={{0,8},{8,0},{1,9},{9,1},{2,10},{10,2},{3,11},{11,3},{4,12},{12,4},... | collective-permute-start | bytes 1769480 | tf_op jit(solution)/shard_map/ppermute | solution.py:28
  54.6 6.5 %collective-permute-start.15 = (bf16[2,256,256]{2,1,0:T(8,128)(2,1)S(1)}, bf16[2,256,256]{2,1,0:T(8,128)(2,1)S(1)}, u32[]{:S(2)}, u32[]{:S(2)}) collective-permute-start(bf16[2,256,256]{2,1,0:T(8,128)(2,1)S(1)} %collective-permute-done.11.refs_3_), channel_id=1, source_target_pairs={{0,16},{16,32},{32,48},{48,64},{64,80},{80,96},{96,112},{112,0},{1... | collective-permute-start | bytes 786440 | tf_op jit(solution)/shard_map/ppermute | solution.py:28
  54.9 6.4 %collective-permute-start.16 = (bf16[2,256,256]{2,1,0:T(8,128)(2,1)S(1)}, bf16[2,256,256]{2,1,0:T(8,128)(2,1)S(1)}, u32[]{:S(2)}, u32[]{:S(2)}) collective-permute-start(bf16[2,256,256]{2,1,0:T(8,128)(2,1)S(1)} %collective-permute-done.11.refs_3_), channel_id=1, source_target_pairs={{0,128},{128,0},{1,129},{129,1},{2,130},{130,2},{3,131},{131,3},{4... | collective-permute-start | bytes 786440 | tf_op jit(solution)/shard_map/ppermute | solution.py:204
  56.0 6.4 %collective-permute-start.17 = (bf16[2,256,256]{2,1,0:T(8,128)(2,1)S(1)}, bf16[2,256,256]{2,1,0:T(8,128)(2,1)S(1)}, u32[]{:S(2)}, u32[]{:S(2)}) collective-permute-start(bf16[2,256,256]{2,1,0:T(8,128)(2,1)S(1)} %collective-permute-done.14.refs_7_), channel_id=1, source_target_pairs={{0,129},{129,0},{1,128},{128,1},{2,131},{131,2},{3,130},{130,3},{4... | collective-permute-start | bytes 786440 | tf_op jit(solution)/shard_map/ppermute | solution.py:204
  62.5 8.3 %collective-permute-start.18 = (bf16[2,256,256]{2,1,0:T(8,128)(2,1)S(1)}, bf16[2,256,256]{2,1,0:T(8,128)(2,1)S(1)}, u32[]{:S(2)}, u32[]{:S(2)}) collective-permute-start(bf16[2,256,256]{2,1,0:T(8,128)(2,1)S(1)} %collective-permute-done.15.refs_4_), channel_id=1, source_target_pairs={{0,129},{129,0},{1,128},{128,1},{2,131},{131,2},{3,130},{130,3},{4... | collective-permute-start | bytes 786440 | tf_op jit(solution)/shard_map/ppermute | solution.py:204
  115.9 23.4 %all-to-all-start.2 = ((bf16[16,128,128]{1,2,0:T(8,128)(2,1)}), bf16[16,128,128]{1,2,0:T(8,128)(2,1)S(1)}, u32[]{:S(2)}, u32[]{:S(2)}) async-start(bf16[16,128,128]{1,2,0:T(8,128)(2,1)} %broadcast_in_dim.11), calls=%async_computation.2 | async-start | bytes 1048576 | tf_op jit(solution)/shard_map/all_to_all | solution.py:18
  140.5 19.5 %all-to-all-start.3 = ((bf16[16,128,128]{2,1,0:T(8,128)(2,1)}), bf16[16,128,128]{2,1,0:T(8,128)(2,1)S(1)}, u32[]{:S(2)}, u32[]{:S(2)}) async-start(bf16[16,128,128]{2,1,0:T(8,128)(2,1)} %broadcast_in_dim.12), calls=%async_computation.3 | async-start | bytes 1048576 | tf_op jit(solution)/shard_map/all_to_all | solution.py:18
  161.2 21.9 %all-to-all-start.4 = ((bf16[16,128,128]{2,1,0:T(8,128)(2,1)}), bf16[16,128,128]{2,1,0:T(8,128)(2,1)S(1)}, u32[]{:S(2)}, u32[]{:S(2)}) async-start(bf16[16,128,128]{2,1,0:T(8,128)(2,1)} %bitcast.18), calls=%async_computation.4 | async-start | bytes 1048576 | tf_op jit(solution)/shard_map/all_to_all | solution.py:18
  167.9 26.3 %collective-permute-start.19 = (bf16[8,2,192,256]{3,2,1,0:T(8,128)(2,1)S(1)}, bf16[8,2,192,256]{3,2,1,0:T(8,128)(2,1)}, u32[]{:S(2)}, u32[]{:S(2)}) collective-permute-start(bf16[8,2,192,256]{3,2,1,0:T(8,128)(2,1)S(1)} %copy-done.4), channel_id=1, source_target_pairs={{0,8},{8,0},{1,9},{9,1},{2,10},{10,2},{3,11},{11,3},{4,12},{12,4},... | collective-permute-start | bytes 4718600 | tf_op jit(solution)/shard_map/ppermute | solution.py:28
  168.9 25.4 %collective-permute-start.20 = (bf16[8,2,192,256]{3,2,1,0:T(8,128)(2,1)}, bf16[8,2,192,256]{3,2,1,0:T(8,128)(2,1)}, u32[]{:S(2)}, u32[]{:S(2)}) collective-permute-start(bf16[8,2,192,256]{3,2,1,0:T(8,128)(2,1)} %get-tuple-element.50.near1), channel_id=1, source_target_pairs={{0,8},{8,0},{1,9},{9,1},{2,10},{10,2},{3,11},{11,3},{4,12},{12,4},... | collective-permute-start | bytes 4718600 | tf_op jit(solution)/shard_map/ppermute | solution.py:28
  188.0 20.9 %all-to-all-start.5 = ((bf16[16,192,128]{2,1,0:T(8,128)(2,1)}), bf16[16,192,128]{2,1,0:T(8,128)(2,1)S(1)}, u32[]{:S(2)}, u32[]{:S(2)}) async-start(bf16[16,192,128]{2,1,0:T(8,128)(2,1)} %half.1), calls=%async_computation.5 | async-start | bytes 1572864 | tf_op jit(solution)/shard_map/all_to_all | solution.py:18
  (27 other events, 536.1 us)
Sparse Core Ops, SparseCore 0:
  46.3 43.6 all-gather.2

commit v5 on v4

--- a/solution.py
+++ b/solution.py
@@ -210,7 +210,8 @@
             moved.append(across(down[d], other_way))
         if d < 3:
             moved.append(shift(down[d], "z", -1))
-        moved = lax.optimization_barrier(moved)
+        if d < 3:
+            moved = lax.optimization_barrier(moved)
         up.append(moved[0])
         mate_up.append(moved[1])
         if d > 0:

time: 224 us -> 225 us (level)
  blocking collectives: 34.9 us -> 42 us
  starting transfers between devices: 70.6 us -> 67 us
  waiting for transfers between devices: 65.8 us -> 63.3 us
    all_to_all x2, blocking collectives: 34.9 us -> 42 us  [swap(): return lax.all_to_all(value, axes, 0, 0, tiled=True)]
    all_to_all x4, starting transfers between devices: 29.6 us -> 25.6 us  [swap(): return lax.all_to_all(value, axes, 0, 0, tiled=True)]
    ppermute x8, waiting for transfers between devices: 3.29 us -> 0.83 us  [across(): return lax.ppermute(value, ('yl', 'tau'), way)]
  transfers between devices with their start and end apart: 26 -> 26, of which waited for: 13 -> 10; matrix products, arithmetic and copies ran while one was open for 3% -> 3% of each run, Pallas kernels for 6% -> 6%
where the time goes in v5:
time: 225 us; the launch traced here: 224 us
  starting transfers between devices  67 us (30%)
  waiting for transfers between devices  63.3 us (28%)
  blocking collectives  42 us (19%)
  Pallas kernels  18.9 us (8%)
  between operations  13.9 us (6%)
  local copies, waits for them, and re-layouts  11.4 us (5%)
  matrix products  4.17 us (2%)
  other arithmetic  3.07 us (1%)
    all_to_all x4, waiting for transfers between devices, swap(): return lax.all_to_all(value, axes, 0, 0, tiled=True)  52.7 us
    all_to_all x2, blocking collectives, swap(): return lax.all_to_all(value, axes, 0, 0, tiled=True)  42 us
    all_to_all x4, starting transfers between devices, swap(): return lax.all_to_all(value, axes, 0, 0, tiled=True)  25.6 us
    ppermute x11, starting transfers between devices, shift(): return lax.ppermute(value, axis, [(i, (i + by) % n) for i in range(n)])  19 us
    ppermute x8, starting transfers between devices, across(): return lax.ppermute(value, ('yl', 'tau'), way)  18.4 us
    ppermute x11, waiting for transfers between devices, shift(): return lax.ppermute(value, axis, [(i, (i + by) % n) for i in range(n)])  9.73 us
    pallas_call x2, Pallas kernels, inner_call(): pl.pallas_call(functools.partial(inner_kernel, second), out_shape=(jax.Sh...  8.71 us
    pallas_call x1, Pallas kernels, sigma_call(): pl.pallas_call(functools.partial(sigma_kernel, scale, rows), out_shape=ja...  6.1 us
  transfers between devices with their start and end apart: 26, of which 10 were waited for; matrix products, arithmetic and copies ran while one was open for 3% of the time, Pallas kernels for 6%

profile of v5, /device:TPU:1, one launch (start us, length us, event | category | flops | bytes accessed | tf_op | source)
XLA Modules:
  0.0 223.8 jit_solution(9334583261163979124)
XLA Ops:
  7.7 3.3 %collective-permute-start.1 = (bf16[192,256]{1,0:T(8,128)(2,1)S(1)}, bf16[192,256]{1,0:T(8,128)(2,1)S(1)}, u32[]{:S(2)}, u32[]{:S(2)}) collective-permute-start(bf16[192,256]{1,0:T(8,128)(2,1)S(1)} %get-tuple-element.46), channel_id=1, source_target_pairs={{0,8},{2,120},{4,136},{6,248},{8,0},{10,112},{12,128},{14,240},{16... | collective-permute-start | bytes 294920 | tf_op jit(solution)/shard_map/ppermute | solution.py:188
  15.9 8.0 %collective-permute-start.4 = (bf16[2,256,256]{2,1,0:T(8,128)(2,1)S(1)}, bf16[2,256,256]{2,1,0:T(8,128)(2,1)S(1)}, u32[]{:S(2)}, u32[]{:S(2)}) collective-permute-start(bf16[2,256,256]{2,1,0:T(8,128)(2,1)S(1)} %maximum_select_fusion.1.refs_0_), channel_id=1, source_target_pairs={{0,128},{128,0},{1,129},{129,1},{2,130},{130,2},{3,131},{131,3},{4... | collective-permute-start | bytes 786440 | tf_op jit(solution)/shard_map/ppermute | solution.py:204
  23.9 7.7 %collective-permute-start.5 = (bf16[2,256,256]{2,1,0:T(8,128)(2,1)S(1)}, bf16[2,256,256]{2,1,0:T(8,128)(2,1)S(1)}, u32[]{:S(2)}, u32[]{:S(2)}) collective-permute-start(bf16[2,256,256]{2,1,0:T(8,128)(2,1)S(1)} %maximum_select_fusion.1.refs_0_), channel_id=1, source_target_pairs={{0,112},{16,0},{32,16},{48,32},{64,48},{80,64},{96,80},{112,96},{1... | collective-permute-start | bytes 786440 | tf_op jit(solution)/shard_map/ppermute | solution.py:28
  31.6 2.8 %collective-permute-done.3.refs_1_ = bf16[2,256,256]{2,1,0:T(8,128)(2,1)S(1)} collective-permute-done((bf16[2,256,256]{2,1,0:T(8,128)(2,1)S(1)}, bf16[2,256,256]{2,1,0:T(8,128)(2,1)S(1)}, u32[]{:S(2)}, u32[]{:S(2)}) %collective-permute-start.3) | collective-permute-done | bytes 262176 | tf_op jit(solution)/shard_map/ppermute | solution.py:28
  39.6 3.3 %collective-permute-start.9 = (bf16[2,256,256]{2,1,0:T(8,128)(2,1)S(1)}, bf16[2,256,256]{2,1,0:T(8,128)(2,1)S(1)}, u32[]{:S(2)}, u32[]{:S(2)}) collective-permute-start(bf16[2,256,256]{2,1,0:T(8,128)(2,1)S(1)} %collective-permute-done.5.refs_5_), channel_id=1, source_target_pairs={{0,112},{16,0},{32,16},{48,32},{64,48},{80,64},{96,80},{112,96},{1... | collective-permute-start | bytes 786440 | tf_op jit(solution)/shard_map/ppermute | solution.py:28
  48.2 2.7 %collective-permute-start.14 = (bf16[2,256,256]{2,1,0:T(8,128)(2,1)S(1)}, bf16[2,256,256]{2,1,0:T(8,128)(2,1)S(1)}, u32[]{:S(2)}, u32[]{:S(2)}) collective-permute-start(bf16[2,256,256]{2,1,0:T(8,128)(2,1)S(1)} %collective-permute-done.9.refs_6_), channel_id=1, source_target_pairs={{0,112},{16,0},{32,16},{48,32},{64,48},{80,64},{96,80},{112,96},{1... | collective-permute-start | bytes 786440 | tf_op jit(solution)/shard_map/ppermute | solution.py:28
  50.8 3.7 %collective-permute-start.10 = (bf16[192,1536]{1,0:T(8,128)(2,1)S(1)}, bf16[192,1536]{1,0:T(8,128)(2,1)S(1)}, u32[]{:S(2)}, u32[]{:S(2)}) collective-permute-start(bf16[192,1536]{1,0:T(8,128)(2,1)S(1)} %reshape.56.own), channel_id=1, source_target_pairs={{0,8},{8,0},{1,9},{9,1},{2,10},{10,2},{3,11},{11,3},{4,12},{12,4},... | collective-permute-start | bytes 1769480 | tf_op jit(solution)/shard_map/ppermute | solution.py:28
  58.0 3.0 %collective-permute-done.16.refs_4_ = bf16[2,256,256]{2,1,0:T(8,128)(2,1)S(1)} collective-permute-done((bf16[2,256,256]{2,1,0:T(8,128)(2,1)S(1)}, bf16[2,256,256]{2,1,0:T(8,128)(2,1)S(1)}, u32[]{:S(2)}, u32[]{:S(2)}) %collective-permute-start.16) | collective-permute-done | bytes 262176 | tf_op jit(solution)/shard_map/ppermute | solution.py:28
  61.1 2.5 %collective-permute-start.17 = (bf16[2,256,256]{2,1,0:T(8,128)(2,1)S(1)}, bf16[2,256,256]{2,1,0:T(8,128)(2,1)S(1)}, u32[]{:S(2)}, u32[]{:S(2)}) collective-permute-start(bf16[2,256,256]{2,1,0:T(8,128)(2,1)S(1)} %collective-permute-done.16.refs_4_), channel_id=1, source_target_pairs={{0,129},{129,0},{1,128},{128,1},{2,131},{131,2},{3,130},{130,3},{4... | collective-permute-start | bytes 786440 | tf_op jit(solution)/shard_map/ppermute | solution.py:204
  64.5 4.2 %inner.2 = (bf16[2,2,2,192,128]{4,3,2,1,0:T(8,128)(2,1)}, bf16[1024,128]{1,0:T(8,128)(2,1)}, bf16[8,2,192,256]{3,2,1,0:T(8,128)(2,1)}) custom-call(bf16[192,1536]{1,0:T(8,128)(2,1)} %copy-done, bf16[192,1536]{1,0:T(8,128)(2,1)} %copy-done.2, bf16[2,256,256]{2,1,0:T(8,128)(2,1)} %copy-done.5, bf16[2,256,256]{2,1,0:T(8,128)(2,1)} %copy-done.15, ...), custom_call_target="tpu_custom_call" | custom-call | flops 603979776 | bytes 6291456 | tf_op jit(solution)/shard_map/inner/pallas_call | solution.py:100
  69.6 4.5 %inner.3 = (bf16[4,2,2,192,128]{4,3,2,1,0:T(8,128)(2,1)}, bf16[1024,128]{1,0:T(8,128)(2,1)}, bf16[8,2,192,256]{3,2,1,0:T(8,128)(2,1)}) custom-call(bf16[192,1536]{1,0:T(8,128)(2,1)} %copy-done, bf16[192,1536]{1,0:T(8,128)(2,1)} %copy-done.2, bf16[2,256,256]{2,1,0:T(8,128)(2,1)} %copy-done.7, bf16[2,256,256]{2,1,0:T(8,128)(2,1)} %copy-done.8, ...), custom_call_target="tpu_custom_call" | custom-call | flops 603979776 | bytes 6291456 | tf_op jit(solution)/shard_map/inner/pallas_call | solution.py:100
  74.1 17.6 %all_to_all.30 = bf16[8,2,192,128]{3,2,1,0:T(8,128)(2,1)S(1)} all-to-all(bf16[8,2,192,128]{3,2,1,0:T(8,128)(2,1)} %bitcast.47), channel_id=1, replica_groups=mesh['yl'=2,'z'=8,'c'=2,'orb'=4,'tau'=2] {'orb','yl'}, dimensions={0} | all-to-all | bytes 1572864 | tf_op jit(solution)/shard_map/all_to_all | solution.py:18
  92.0 3.5 %convolution_convert_fusion = bf16[4,512,128]{2,1,0:T(8,128)(2,1)S(1)} fusion(bf16[4,1024,512]{2,1,0:T(8,128)(2,1)} %bitcast.37, bf16[1024,128,1]{1,0,2:T(8,128)(2,1)S(1)} %bitcast.49), kind=kOutput, calls=%fused_computation | convolution fusion | flops 537133056 | bytes 4980736 | tf_op jit(solution)/shard_map/dot_general | solution.py:242
  95.6 24.4 %all_to_all.31 = bf16[16,128,128]{2,1,0:T(8,128)(2,1)S(1)} all-to-all(bf16[16,128,128]{2,1,0:T(8,128)(2,1)S(1)} %bitcast.48), channel_id=1, replica_groups=mesh['yl'=2,'z'=8,'c'=2,'orb'=4,'tau'=2] {'tau','z'}, dimensions={0} | all-to-all | bytes 1048576 | tf_op jit(solution)/shard_map/all_to_all | solution.py:18
  121.1 7.8 %all-to-all-start.2 = ((bf16[16,128,128]{1,2,0:T(8,128)(2,1)}), bf16[16,128,128]{1,2,0:T(8,128)(2,1)S(1)}, u32[]{:S(2)}, u32[]{:S(2)}) async-start(bf16[16,128,128]{1,2,0:T(8,128)(2,1)} %broadcast_in_dim.11), calls=%async_computation.2 | async-start | bytes 1048576 | tf_op jit(solution)/shard_map/all_to_all | solution.py:18
  129.0 10.9 %all-to-all-done.2 = bf16[16,128,128]{1,2,0:T(8,128)(2,1)S(1)} async-done(((bf16[16,128,128]{1,2,0:T(8,128)(2,1)}), bf16[16,128,128]{1,2,0:T(8,128)(2,1)S(1)}, u32[]{:S(2)}, u32[]{:S(2)}) %all-to-all-start.2) | async-done | bytes 524320 | tf_op jit(solution)/shard_map/all_to_all | solution.py:18
  141.2 4.7 %all-to-all-start.3 = ((bf16[16,128,128]{2,1,0:T(8,128)(2,1)}), bf16[16,128,128]{2,1,0:T(8,128)(2,1)S(1)}, u32[]{:S(2)}, u32[]{:S(2)}) async-start(bf16[16,128,128]{2,1,0:T(8,128)(2,1)} %broadcast_in_dim.12), calls=%async_computation.3 | async-start | bytes 1048576 | tf_op jit(solution)/shard_map/all_to_all | solution.py:18
  148.0 13.1 %all-to-all-done.3 = bf16[16,128,128]{2,1,0:T(8,128)(2,1)S(1)} async-done(((bf16[16,128,128]{2,1,0:T(8,128)(2,1)}), bf16[16,128,128]{2,1,0:T(8,128)(2,1)S(1)}, u32[]{:S(2)}, u32[]{:S(2)}) %all-to-all-start.3) | async-done | bytes 524320 | tf_op jit(solution)/shard_map/all_to_all | solution.py:18
  162.3 6.7 %all-to-all-start.4 = ((bf16[16,128,128]{2,1,0:T(8,128)(2,1)}), bf16[16,128,128]{2,1,0:T(8,128)(2,1)S(1)}, u32[]{:S(2)}, u32[]{:S(2)}) async-start(bf16[16,128,128]{2,1,0:T(8,128)(2,1)} %bitcast.18), calls=%async_computation.4 | async-start | bytes 1048576 | tf_op jit(solution)/shard_map/all_to_all | solution.py:18
  170.1 14.1 %all-to-all-done.4 = bf16[16,128,128]{2,1,0:T(8,128)(2,1)S(1)} async-done(((bf16[16,128,128]{2,1,0:T(8,128)(2,1)}), bf16[16,128,128]{2,1,0:T(8,128)(2,1)S(1)}, u32[]{:S(2)}, u32[]{:S(2)}) %all-to-all-start.4) | async-done | bytes 524320 | tf_op jit(solution)/shard_map/all_to_all | solution.py:18
  184.9 4.1 %half.1 = bf16[16,192,128]{2,1,0:T(8,128)(2,1)} custom-call(bf16[4,4,256,512]{3,2,1,0:T(8,128)(2,1)} %bitcast.39, bf16[4,512,128]{2,1,0:T(8,128)(2,1)} %bitcast.46), custom_call_target="tpu_custom_call" | custom-call | flops 402653184 | bytes 5242880 | tf_op jit(solution)/shard_map/half/pallas_call | solution.py:122
  189.1 6.3 %all-to-all-start.5 = ((bf16[16,192,128]{2,1,0:T(8,128)(2,1)}), bf16[16,192,128]{2,1,0:T(8,128)(2,1)S(1)}, u32[]{:S(2)}, u32[]{:S(2)}) async-start(bf16[16,192,128]{2,1,0:T(8,128)(2,1)} %half.1), calls=%async_computation.5 | async-start | bytes 1572864 | tf_op jit(solution)/shard_map/all_to_all | solution.py:18
  195.3 14.7 %all-to-all-done.5.h = bf16[16,192,128]{2,1,0:T(8,128)(2,1)S(1)} async-done(((bf16[16,192,128]{2,1,0:T(8,128)(2,1)}), bf16[16,192,128]{2,1,0:T(8,128)(2,1)S(1)}, u32[]{:S(2)}, u32[]{:S(2)}) %all-to-all-start.5) | async-done | bytes 786464 | tf_op jit(solution)/shard_map/all_to_all | solution.py:18
  210.9 6.1 %sigma.1 = bf16[188,1504]{1,0:T(8,128)(2,1)} custom-call(bf16[16,192,128]{2,1,0:T(8,128)(2,1)} %copy-done.1, bf16[8,2,192,256]{3,2,1,0:T(8,128)(2,1)} %get-tuple-element.43.near0, bf16[8,2,192,256]{3,2,1,0:T(8,128)(2,1)} %get-tuple-element.44.near1, bf16[8,2,192,256]{3,2,1,0:T(8,128)(2,1)} %collective-permute-done.19.far0, ...), custom_call_target="tpu_custom_call" | custom-call | flops 1207959552 | bytes 8388608 | tf_op jit(solution)/shard_map/sigma/pallas_call | solution.py:151
  (114 shorter events, 30.2 us)
Async XLA Ops:
  6.5 85.5 %all-gather.3.cloned.1.call-start = ((), (), s32[]{:S(2)}) async-start(), calls=%async_computation.6 | async-start | bytes 4456448 | tf_op jit(solution)/shard_map/all_gather | solution.py:226
  7.7 8.1 %collective-permute-start.1 = (bf16[192,256]{1,0:T(8,128)(2,1)S(1)}, bf16[192,256]{1,0:T(8,128)(2,1)S(1)}, u32[]{:S(2)}, u32[]{:S(2)}) collective-permute-start(bf16[192,256]{1,0:T(8,128)(2,1)S(1)} %get-tuple-element.46), channel_id=1, source_target_pairs={{0,8},{2,120},{4,136},{6,248},{8,0},{10,112},{12,128},{14,240},{16... | collective-permute-start | bytes 294920 | tf_op jit(solution)/shard_map/ppermute | solution.py:188
  15.9 18.6 %collective-permute-start.3 = (bf16[2,256,256]{2,1,0:T(8,128)(2,1)S(1)}, bf16[2,256,256]{2,1,0:T(8,128)(2,1)S(1)}, u32[]{:S(2)}, u32[]{:S(2)}) collective-permute-start(bf16[2,256,256]{2,1,0:T(8,128)(2,1)S(1)} %maximum_select_fusion.1.refs_0_), channel_id=1, source_target_pairs={{0,16},{16,32},{32,48},{48,64},{64,80},{80,96},{96,112},{112,0},{1... | collective-permute-start | bytes 786440 | tf_op jit(solution)/shard_map/ppermute | solution.py:28
  15.9 18.5 %collective-permute-start.4 = (bf16[2,256,256]{2,1,0:T(8,128)(2,1)S(1)}, bf16[2,256,256]{2,1,0:T(8,128)(2,1)S(1)}, u32[]{:S(2)}, u32[]{:S(2)}) collective-permute-start(bf16[2,256,256]{2,1,0:T(8,128)(2,1)S(1)} %maximum_select_fusion.1.refs_0_), channel_id=1, source_target_pairs={{0,128},{128,0},{1,129},{129,1},{2,130},{130,2},{3,131},{131,3},{4... | collective-permute-start | bytes 786440 | tf_op jit(solution)/shard_map/ppermute | solution.py:204
  23.9 12.7 %collective-permute-start.5 = (bf16[2,256,256]{2,1,0:T(8,128)(2,1)S(1)}, bf16[2,256,256]{2,1,0:T(8,128)(2,1)S(1)}, u32[]{:S(2)}, u32[]{:S(2)}) collective-permute-start(bf16[2,256,256]{2,1,0:T(8,128)(2,1)S(1)} %maximum_select_fusion.1.refs_0_), channel_id=1, source_target_pairs={{0,112},{16,0},{32,16},{48,32},{64,48},{80,64},{96,80},{112,96},{1... | collective-permute-start | bytes 786440 | tf_op jit(solution)/shard_map/ppermute | solution.py:28
  36.6 8.5 %collective-permute-start.6 = (bf16[2,256,256]{2,1,0:T(8,128)(2,1)S(1)}, bf16[2,256,256]{2,1,0:T(8,128)(2,1)S(1)}, u32[]{:S(2)}, u32[]{:S(2)}) collective-permute-start(bf16[2,256,256]{2,1,0:T(8,128)(2,1)S(1)} %collective-permute-done.3.refs_1_), channel_id=1, source_target_pairs={{0,16},{16,32},{32,48},{48,64},{64,80},{80,96},{96,112},{112,0},{1... | collective-permute-start | bytes 786440 | tf_op jit(solution)/shard_map/ppermute | solution.py:28
  36.6 8.5 %collective-permute-start.7 = (bf16[2,256,256]{2,1,0:T(8,128)(2,1)S(1)}, bf16[2,256,256]{2,1,0:T(8,128)(2,1)S(1)}, u32[]{:S(2)}, u32[]{:S(2)}) collective-permute-start(bf16[2,256,256]{2,1,0:T(8,128)(2,1)S(1)} %collective-permute-done.3.refs_1_), channel_id=1, source_target_pairs={{0,128},{128,0},{1,129},{129,1},{2,130},{130,2},{3,131},{131,3},{4... | collective-permute-start | bytes 786440 | tf_op jit(solution)/shard_map/ppermute | solution.py:204
  38.0 7.8 %collective-permute-start.8 = (bf16[2,256,256]{2,1,0:T(8,128)(2,1)S(1)}, bf16[2,256,256]{2,1,0:T(8,128)(2,1)S(1)}, u32[]{:S(2)}, u32[]{:S(2)}) collective-permute-start(bf16[2,256,256]{2,1,0:T(8,128)(2,1)S(1)} %collective-permute-done.5.refs_5_), channel_id=1, source_target_pairs={{0,129},{129,0},{1,128},{128,1},{2,131},{131,2},{3,130},{130,3},{4... | collective-permute-start | bytes 786440 | tf_op jit(solution)/shard_map/ppermute | solution.py:204
  39.6 6.6 %collective-permute-start.9 = (bf16[2,256,256]{2,1,0:T(8,128)(2,1)S(1)}, bf16[2,256,256]{2,1,0:T(8,128)(2,1)S(1)}, u32[]{:S(2)}, u32[]{:S(2)}) collective-permute-start(bf16[2,256,256]{2,1,0:T(8,128)(2,1)S(1)} %collective-permute-done.5.refs_5_), channel_id=1, source_target_pairs={{0,112},{16,0},{32,16},{48,32},{64,48},{80,64},{96,80},{112,96},{1... | collective-permute-start | bytes 786440 | tf_op jit(solution)/shard_map/ppermute | solution.py:28
  46.2 8.3 %collective-permute-start.11 = (bf16[2,256,256]{2,1,0:T(8,128)(2,1)S(1)}, bf16[2,256,256]{2,1,0:T(8,128)(2,1)S(1)}, u32[]{:S(2)}, u32[]{:S(2)}) collective-permute-start(bf16[2,256,256]{2,1,0:T(8,128)(2,1)S(1)} %collective-permute-done.6.refs_2_), channel_id=1, source_target_pairs={{0,16},{16,32},{32,48},{48,64},{64,80},{80,96},{96,112},{112,0},{1... | collective-permute-start | bytes 786440 | tf_op jit(solution)/shard_map/ppermute | solution.py:28
  46.3 8.2 %collective-permute-start.12 = (bf16[2,256,256]{2,1,0:T(8,128)(2,1)S(1)}, bf16[2,256,256]{2,1,0:T(8,128)(2,1)S(1)}, u32[]{:S(2)}, u32[]{:S(2)}) collective-permute-start(bf16[2,256,256]{2,1,0:T(8,128)(2,1)S(1)} %collective-permute-done.6.refs_2_), channel_id=1, source_target_pairs={{0,128},{128,0},{1,129},{129,1},{2,130},{130,2},{3,131},{131,3},{4... | collective-permute-start | bytes 786440 | tf_op jit(solution)/shard_map/ppermute | solution.py:204
  46.9 7.6 %collective-permute-start.13 = (bf16[2,256,256]{2,1,0:T(8,128)(2,1)S(1)}, bf16[2,256,256]{2,1,0:T(8,128)(2,1)S(1)}, u32[]{:S(2)}, u32[]{:S(2)}) collective-permute-start(bf16[2,256,256]{2,1,0:T(8,128)(2,1)S(1)} %collective-permute-done.9.refs_6_), channel_id=1, source_target_pairs={{0,129},{129,0},{1,128},{128,1},{2,131},{131,2},{3,130},{130,3},{4... | collective-permute-start | bytes 786440 | tf_op jit(solution)/shard_map/ppermute | solution.py:204
  48.2 6.4 %collective-permute-start.14 = (bf16[2,256,256]{2,1,0:T(8,128)(2,1)S(1)}, bf16[2,256,256]{2,1,0:T(8,128)(2,1)S(1)}, u32[]{:S(2)}, u32[]{:S(2)}) collective-permute-start(bf16[2,256,256]{2,1,0:T(8,128)(2,1)S(1)} %collective-permute-done.9.refs_6_), channel_id=1, source_target_pairs={{0,112},{16,0},{32,16},{48,32},{64,48},{80,64},{96,80},{112,96},{1... | collective-permute-start | bytes 786440 | tf_op jit(solution)/shard_map/ppermute | solution.py:28
  50.8 12.7 %collective-permute-start.10 = (bf16[192,1536]{1,0:T(8,128)(2,1)S(1)}, bf16[192,1536]{1,0:T(8,128)(2,1)S(1)}, u32[]{:S(2)}, u32[]{:S(2)}) collective-permute-start(bf16[192,1536]{1,0:T(8,128)(2,1)S(1)} %reshape.56.own), channel_id=1, source_target_pairs={{0,8},{8,0},{1,9},{9,1},{2,10},{10,2},{3,11},{11,3},{4,12},{12,4},... | collective-permute-start | bytes 1769480 | tf_op jit(solution)/shard_map/ppermute | solution.py:28
  54.6 6.5 %collective-permute-start.16 = (bf16[2,256,256]{2,1,0:T(8,128)(2,1)S(1)}, bf16[2,256,256]{2,1,0:T(8,128)(2,1)S(1)}, u32[]{:S(2)}, u32[]{:S(2)}) collective-permute-start(bf16[2,256,256]{2,1,0:T(8,128)(2,1)S(1)} %collective-permute-done.11.refs_3_), channel_id=1, source_target_pairs={{0,16},{16,32},{32,48},{48,64},{64,80},{80,96},{96,112},{112,0},{1... | collective-permute-start | bytes 786440 | tf_op jit(solution)/shard_map/ppermute | solution.py:28
  54.9 13.8 %collective-permute-start.15 = (bf16[2,256,256]{2,1,0:T(8,128)(2,1)S(1)}, bf16[2,256,256]{2,1,0:T(8,128)(2,1)S(1)}, u32[]{:S(2)}, u32[]{:S(2)}) collective-permute-start(bf16[2,256,256]{2,1,0:T(8,128)(2,1)S(1)} %collective-permute-done.11.refs_3_), channel_id=1, source_target_pairs={{0,128},{128,0},{1,129},{129,1},{2,130},{130,2},{3,131},{131,3},{4... | collective-permute-start | bytes 786440 | tf_op jit(solution)/shard_map/ppermute | solution.py:204
  56.0 12.7 %collective-permute-start.18 = (bf16[2,256,256]{2,1,0:T(8,128)(2,1)S(1)}, bf16[2,256,256]{2,1,0:T(8,128)(2,1)S(1)}, u32[]{:S(2)}, u32[]{:S(2)}) collective-permute-start(bf16[2,256,256]{2,1,0:T(8,128)(2,1)S(1)} %collective-permute-done.14.refs_7_), channel_id=1, source_target_pairs={{0,129},{129,0},{1,128},{128,1},{2,131},{131,2},{3,130},{130,3},{4... | collective-permute-start | bytes 786440 | tf_op jit(solution)/shard_map/ppermute | solution.py:204
  61.1 7.6 %collective-permute-start.17 = (bf16[2,256,256]{2,1,0:T(8,128)(2,1)S(1)}, bf16[2,256,256]{2,1,0:T(8,128)(2,1)S(1)}, u32[]{:S(2)}, u32[]{:S(2)}) collective-permute-start(bf16[2,256,256]{2,1,0:T(8,128)(2,1)S(1)} %collective-permute-done.16.refs_4_), channel_id=1, source_target_pairs={{0,129},{129,0},{1,128},{128,1},{2,131},{131,2},{3,130},{130,3},{4... | collective-permute-start | bytes 786440 | tf_op jit(solution)/shard_map/ppermute | solution.py:204
  121.1 18.9 %all-to-all-start.2 = ((bf16[16,128,128]{1,2,0:T(8,128)(2,1)}), bf16[16,128,128]{1,2,0:T(8,128)(2,1)S(1)}, u32[]{:S(2)}, u32[]{:S(2)}) async-start(bf16[16,128,128]{1,2,0:T(8,128)(2,1)} %broadcast_in_dim.11), calls=%async_computation.2 | async-start | bytes 1048576 | tf_op jit(solution)/shard_map/all_to_all | solution.py:18
  141.2 19.9 %all-to-all-start.3 = ((bf16[16,128,128]{2,1,0:T(8,128)(2,1)}), bf16[16,128,128]{2,1,0:T(8,128)(2,1)S(1)}, u32[]{:S(2)}, u32[]{:S(2)}) async-start(bf16[16,128,128]{2,1,0:T(8,128)(2,1)} %broadcast_in_dim.12), calls=%async_computation.3 | async-start | bytes 1048576 | tf_op jit(solution)/shard_map/all_to_all | solution.py:18
  162.3 21.9 %all-to-all-start.4 = ((bf16[16,128,128]{2,1,0:T(8,128)(2,1)}), bf16[16,128,128]{2,1,0:T(8,128)(2,1)S(1)}, u32[]{:S(2)}, u32[]{:S(2)}) async-start(bf16[16,128,128]{2,1,0:T(8,128)(2,1)} %bitcast.18), calls=%async_computation.4 | async-start | bytes 1048576 | tf_op jit(solution)/shard_map/all_to_all | solution.py:18
  169.0 26.3 %collective-permute-start.19 = (bf16[8,2,192,256]{3,2,1,0:T(8,128)(2,1)S(1)}, bf16[8,2,192,256]{3,2,1,0:T(8,128)(2,1)}, u32[]{:S(2)}, u32[]{:S(2)}) collective-permute-start(bf16[8,2,192,256]{3,2,1,0:T(8,128)(2,1)S(1)} %copy-done.4), channel_id=1, source_target_pairs={{0,8},{8,0},{1,9},{9,1},{2,10},{10,2},{3,11},{11,3},{4,12},{12,4},... | collective-permute-start | bytes 4718600 | tf_op jit(solution)/shard_map/ppermute | solution.py:28
  170.0 25.4 %collective-permute-start.20 = (bf16[8,2,192,256]{3,2,1,0:T(8,128)(2,1)}, bf16[8,2,192,256]{3,2,1,0:T(8,128)(2,1)}, u32[]{:S(2)}, u32[]{:S(2)}) collective-permute-start(bf16[8,2,192,256]{3,2,1,0:T(8,128)(2,1)} %get-tuple-element.44.near1), channel_id=1, source_target_pairs={{0,8},{8,0},{1,9},{9,1},{2,10},{10,2},{3,11},{11,3},{4,12},{12,4},... | collective-permute-start | bytes 4718600 | tf_op jit(solution)/shard_map/ppermute | solution.py:28
  189.1 20.9 %all-to-all-start.5 = ((bf16[16,192,128]{2,1,0:T(8,128)(2,1)}), bf16[16,192,128]{2,1,0:T(8,128)(2,1)S(1)}, u32[]{:S(2)}, u32[]{:S(2)}) async-start(bf16[16,192,128]{2,1,0:T(8,128)(2,1)} %half.1), calls=%async_computation.5 | async-start | bytes 1572864 | tf_op jit(solution)/shard_map/all_to_all | solution.py:18
  (27 other events, 500.0 us)
Sparse Core Ops, SparseCore 0:
  46.3 44.6 all-gather.2
